TPU v7x, 128 devices: a whole 4x4x4 slice. The times are simulated.
128 devices in a mesh: section: 8 (over y, core), dp: 16 (over z, x).
Axes of the slice: x: 4, y: 4, z: 4, core: 2. Of those that a mesh axis runs over, the one named last changes fastest.
Arguments:
- tokens_in: bfloat16 [2048, 2048], P('dp'), may hold values from -20 to 20
- cotangent: bfloat16 [2048, 2048], P('dp'), may hold values from -6 to 6
- in_weights: bfloat16 [8, 2048, 3072], P('section'), may hold values from -5 to 5, as said below
- out_weights: bfloat16 [8, 1024, 2048], P('section'), may hold values from -0.1875 to 0.1875
- slice_lengths: int32 [16, 8], P('dp'), may hold values from 1 to 32, 128 in all within a row
Outputs:
- section_outputs: bfloat16 [8, 2048, 2048], P('section', 'dp')
- input_grads: bfloat16 [8, 2048, 2048], P('section', 'dp')
- grad_in_weights: bfloat16 [8, 2048, 3072], P('section', 'dp')
- grad_out_weights: bfloat16 [8, 1024, 2048], P('section', None, 'dp')
Inputs may be any that keep to these rules, and one draw needn't show every extreme that they name: `slice_lengths`: each row holds the 8 slice lengths of one sequence in order; they sum to 128 and the longest is exactly 32. `in_weights`: projections of queries, keys and values, in that order along the last dimension.
All inputs are finite; a program needn't handle non-finite values.
Results may differ from a plain program's by a relative error of at most 0.034.
Values may be sent and summed in bfloat16 or wider, within the bound.
A program may use at most 192 MiB of HBM per device.

v0:
```python
import math

import jax
import jax.numpy as jnp
from jax import lax
from jax.sharding import PartitionSpec as P

HS = 128
MOST = 32


def shifted_2(shard, axis, by):
    devices = lax.axis_size(axis)
    pairs = [(i, i + by) for i in range(devices) if 0 <= i + by < devices]
    return lax.ppermute(shard, axis, pairs)


def normalize(block_input):
    values = block_input.astype(jnp.float32)
    centre = jnp.mean(values, -1, keepdims=True)
    shifted = values - centre
    inv_std = lax.rsqrt(jnp.mean(shifted * shifted, -1, keepdims=True) + 1e-05)
    return (shifted * inv_std, inv_std)


def attend(queries, cached_keys, query_pos, key_pos, head_count):
    row_count = queries.shape[0]
    key_count = cached_keys.shape[0]
    head_size = queries.shape[1] // head_count
    scores = jnp.einsum(
        "qhd,khd->hqk",
        queries.reshape(row_count, head_count, head_size),
        cached_keys.reshape(key_count, head_count, head_size),
        preferred_element_type=jnp.float32,
    ) / math.sqrt(head_size)
    scores = jnp.where(key_pos[None, None, :] <= query_pos[None, :, None], scores, -jnp.inf)
    return jax.nn.softmax(scores, axis=-1)


def contract_rows(left, right):
    return lax.dot_general(
        left, right, (((0,), (0,)), ((), ())), preferred_element_type=jnp.float32
    )


def contract_cols(left, right):
    return lax.dot_general(
        left, right, (((1,), (1,)), ((), ())), preferred_element_type=jnp.float32
    )


def on_device(tokens_in, cotangent, in_weights, out_weights, slice_lengths):
    sections = lax.axis_size("section")
    section_index = lax.axis_index("section")
    weight_in = in_weights[0]
    weight_out = out_weights[0]
    seq_len, width = tokens_in.shape
    inner_width = weight_out.shape[0]
    head_count = inner_width // HS
    lengths = slice_lengths[0]
    slice_count = lengths.shape[0]
    slice_ends = jnp.cumsum(lengths)
    block_rows = MOST
    block_starts = slice_ends - lengths
    padded_len = seq_len + block_rows
    positions = jnp.arange(padded_len, dtype=jnp.int32)
    row_offsets = jnp.arange(block_rows, dtype=jnp.int32)
    slice_of = jnp.sum((positions[:, None] >= slice_ends[None, :]).astype(jnp.int32), 1)
    padded_in = jnp.pad(tokens_in, ((0, block_rows), (0, 0)))
    padded_cot = jnp.pad(cotangent, ((0, block_rows), (0, 0)))
    zero_rows = jnp.zeros((block_rows, width), jnp.bfloat16)

    def forward_step(step_num, carried):
        incoming, in_buf, out_buf, proj_buf, mixed_buf = carried
        slot_index = step_num - section_index
        active = (slot_index >= 0) & (slot_index < slice_count)
        clipped = jnp.clip(slot_index, 0, slice_count - 1)
        row_start = block_starts[clipped]
        from_input = lax.dynamic_slice_in_dim(padded_in, row_start, block_rows, 0)
        block_input = jnp.where(section_index == 0, from_input, incoming)

        def forward_compute_block(buffers):
            in_buf, out_buf, proj_buf, mixed_buf = buffers
            x_hat, inv_std = normalize(block_input)
            normed = x_hat.astype(jnp.bfloat16)
            projected = jnp.dot(normed, weight_in, preferred_element_type=jnp.float32).astype(
                jnp.bfloat16
            )
            proj_buf = lax.dynamic_update_slice_in_dim(proj_buf, projected, row_start, 0)
            cached_keys = proj_buf[:, inner_width : 2 * inner_width]
            cached_values = proj_buf[:, 2 * inner_width :].reshape(padded_len, head_count, HS)
            attn_probs = attend(
                projected[:, :inner_width],
                cached_keys,
                row_start + row_offsets,
                positions,
                head_count,
            )
            mixed_heads = jnp.einsum(
                "hqk,khd->qhd",
                attn_probs.astype(jnp.bfloat16),
                cached_values,
                preferred_element_type=jnp.float32,
            )
            mixed_heads = mixed_heads.reshape(block_rows, inner_width).astype(jnp.bfloat16)
            result = (
                block_input.astype(jnp.float32)
                + jnp.dot(mixed_heads, weight_out, preferred_element_type=jnp.float32)
            ).astype(jnp.bfloat16)
            in_buf = lax.dynamic_update_slice_in_dim(in_buf, block_input, row_start, 0)
            out_buf = lax.dynamic_update_slice_in_dim(out_buf, result, row_start, 0)
            mixed_buf = lax.dynamic_update_slice_in_dim(mixed_buf, mixed_heads, row_start, 0)
            return ((in_buf, out_buf, proj_buf, mixed_buf), result)

        def forward_skip_block(buffers):
            return (buffers, zero_rows)

        buffers, result = lax.cond(
            active,
            forward_compute_block,
            forward_skip_block,
            (in_buf, out_buf, proj_buf, mixed_buf),
        )
        incoming = shifted_2(result, "section", 1)
        return (incoming,) + tuple(buffers)

    forward_init = (
        zero_rows,
        jnp.zeros((padded_len, width), jnp.bfloat16),
        jnp.zeros((padded_len, width), jnp.bfloat16),
        jnp.zeros((padded_len, 3 * inner_width), jnp.bfloat16),
        jnp.zeros((padded_len, inner_width), jnp.bfloat16),
    )
    _, in_buf, out_buf, proj_buf, mixed_buf = lax.fori_loop(
        0, slice_count + sections - 1, forward_step, forward_init
    )
    cached_keys = proj_buf[:, inner_width : 2 * inner_width]
    cached_values = proj_buf[:, 2 * inner_width :].reshape(padded_len, head_count, HS)
    zero_b = jnp.zeros((), jnp.bfloat16)

    def backward_step(step_num, carried):
        incoming, grad_buf, grad_proj_buf, normed_buf, cot_buf, key_acc, val_acc = carried
        slot_index = step_num - (sections - 1 - section_index)
        active = (slot_index >= 0) & (slot_index < slice_count)
        block_id = slice_count - 1 - jnp.clip(slot_index, 0, slice_count - 1)
        row_start = block_starts[block_id]
        live_rows = (row_offsets < lengths[block_id])[:, None]
        from_input = lax.dynamic_slice_in_dim(padded_cot, row_start, block_rows, 0)
        upstream = jnp.where(section_index == sections - 1, from_input, incoming)

        def place(buffer, new_rows):
            previous = lax.dynamic_slice_in_dim(buffer, row_start, block_rows, 0)
            return lax.dynamic_update_slice_in_dim(
                buffer, jnp.where(live_rows, new_rows, previous), row_start, 0
            )

        def backward_compute_block(buffers):
            grad_buf, grad_proj_buf, normed_buf, cot_buf, key_acc, val_acc = buffers
            upstream_live = jnp.where(live_rows, upstream, zero_b)
            block_input = lax.dynamic_slice_in_dim(in_buf, row_start, block_rows, 0)
            x_hat, inv_std = normalize(block_input)
            normed = x_hat.astype(jnp.bfloat16)
            queries = lax.dynamic_slice_in_dim(proj_buf, row_start, block_rows, 0)[:, :inner_width]
            attn_probs = attend(
                queries, cached_keys, row_start + row_offsets, positions, head_count
            )
            probs_b = attn_probs.astype(jnp.bfloat16)
            grad_mixed = (
                contract_cols(upstream_live, weight_out)
                .astype(jnp.bfloat16)
                .reshape(block_rows, head_count, HS)
            )
            grad_probs = jnp.einsum(
                "qhd,khd->hqk", grad_mixed, cached_values, preferred_element_type=jnp.float32
            )
            row_delta = jnp.sum(attn_probs * grad_probs, -1, keepdims=True)
            grad_scores = (attn_probs * (grad_probs - row_delta)).astype(jnp.bfloat16)
            key_heads = cached_keys.reshape(padded_len, head_count, HS)
            grad_queries = jnp.einsum(
                "hqk,khd->qhd", grad_scores, key_heads, preferred_element_type=jnp.float32
            ) / math.sqrt(HS)
            query_slices = lax.dynamic_slice_in_dim(slice_of, row_start, block_rows, 0)
            same_slice = (query_slices[:, None] == slice_of[None, :])[None]
            query_heads = queries.reshape(block_rows, head_count, HS)
            key_acc = key_acc + jnp.einsum(
                "hqk,qhd->khd",
                jnp.where(same_slice, grad_scores, zero_b),
                query_heads,
                preferred_element_type=jnp.float32,
            ).reshape(padded_len, inner_width)
            val_acc = val_acc + jnp.einsum(
                "hqk,qhd->khd",
                jnp.where(same_slice, probs_b, zero_b),
                grad_mixed,
                preferred_element_type=jnp.float32,
            ).reshape(padded_len, inner_width)
            grad_keys = lax.dynamic_slice_in_dim(key_acc, row_start, block_rows, 0) / math.sqrt(HS)
            grad_values = lax.dynamic_slice_in_dim(val_acc, row_start, block_rows, 0)
            grad_proj = jnp.concatenate(
                [grad_queries.reshape(block_rows, inner_width), grad_keys, grad_values], 1
            ).astype(jnp.bfloat16)
            grad_normed = contract_cols(grad_proj, weight_in)
            norm_grad = inv_std * (
                grad_normed
                - jnp.mean(grad_normed, -1, keepdims=True)
                - x_hat * jnp.mean(grad_normed * x_hat, -1, keepdims=True)
            )
            grad_input = (upstream_live.astype(jnp.float32) + norm_grad).astype(jnp.bfloat16)
            grad_buf = place(grad_buf, grad_input)
            grad_proj_buf = place(grad_proj_buf, grad_proj)
            normed_buf = place(normed_buf, normed)
            cot_buf = place(cot_buf, upstream_live)
            return ((grad_buf, grad_proj_buf, normed_buf, cot_buf, key_acc, val_acc), grad_input)

        def backward_skip_block(buffers):
            return (buffers, zero_rows)

        buffers, grad_input = lax.cond(
            active,
            backward_compute_block,
            backward_skip_block,
            (grad_buf, grad_proj_buf, normed_buf, cot_buf, key_acc, val_acc),
        )
        incoming = shifted_2(grad_input, "section", -1)
        return (incoming,) + tuple(buffers)

    backward_init = (
        zero_rows,
        jnp.zeros((padded_len, width), jnp.bfloat16),
        jnp.zeros((padded_len, 3 * inner_width), jnp.bfloat16),
        jnp.zeros((padded_len, width), jnp.bfloat16),
        jnp.zeros((padded_len, width), jnp.bfloat16),
        jnp.zeros((padded_len, inner_width), jnp.float32),
        jnp.zeros((padded_len, inner_width), jnp.float32),
    )
    _, grad_buf, grad_proj_buf, normed_buf, cot_buf, _, _ = lax.fori_loop(
        0, slice_count + sections - 1, backward_step, backward_init
    )
    normed_all = normed_buf[:seq_len]
    grad_proj_all = grad_proj_buf[:seq_len]
    cot_all = cot_buf[:seq_len]
    mixed_all = mixed_buf[:seq_len]
    grad_scale = 1.0 / math.sqrt(seq_len * lax.axis_size("dp"))
    term_in = contract_rows(normed_all, grad_proj_all) * grad_scale
    term_out = contract_rows(mixed_all, cot_all) * grad_scale
    grad_in, grad_out = (
        lax.psum_scatter(
            term_in.astype(jnp.bfloat16), "dp", scatter_dimension=0, tiled=True
        ).astype(jnp.float32),
        lax.psum_scatter(
            term_out.astype(jnp.bfloat16), "dp", scatter_dimension=1, tiled=True
        ).astype(jnp.float32),
    )
    return (
        out_buf[None, :seq_len],
        grad_buf[None, :seq_len],
        grad_in.astype(jnp.bfloat16)[None],
        grad_out.astype(jnp.bfloat16)[None],
    )


def solution(mesh):
    placed = (
        P("dp", None),
        P("dp", None),
        P("section", None, None),
        P("section", None, None),
        P("dp", None),
    )
    return jax.shard_map(
        on_device,
        mesh=mesh,
        in_specs=placed,
        out_specs=(
            P("section", "dp", None),
            P("section", "dp", None),
            P("section", "dp", None),
            P("section", None, "dp"),
        ),
        check_vma=False,
    )
```

profile of v0, /device:TPU:0, one launch (start us, length us, event | category | flops | bytes accessed | tf_op | source)
XLA Modules:
  0.0 1347.3 jit_solution(13532072318171604808)
XLA Ops:
  13.7 349.9 %while.52 = (s32[]{:T(128)}, bf16[32,2048]{1,0:T(8,128)(2,1)S(1)}, bf16[160,2048]{1,0:T(8,128)(2,1)}, bf16[160,2048]{1,0:T(8,128)(2,1)}, bf16[160,3072]{1,0:T(8,...) while((s32[]{:T(128)}, bf16[32,2048]{1,0:T(8,128)(2,1)S(1)}, ...), condition=%wide.region_8.9_spmd.clone, body=%wide.region_1.8_spmd.clone.sunk | while | flops 559183488 | bytes 22268268 | solution.py:134
  13.7 22.4 %conditional.7 = (bf16[160,2048]{1,0:T(8,128)(2,1)}, bf16[160,2048]{1,0:T(8,128)(2,1)}, bf16[160,3072]{1,0:T(8,128)(2,1)S(1)}, bf16[160,1024]{1,0:T(8,128)(2,1)}, bf16[32,2048]{1,0:T(8,128)(2,1)}) conditional(s32[]{:T(128)} %convert_element_type.198, (bf16[160,2048]{1,0:T(8,128)(2,1)}, bf16[160,2048]{1,0:T(8,128)(2,1)}, ...), branch_computations={%region_2.2_spmd, %region_3.7_spmd} | conditional | flops 559183488 | bytes 21742856 | solution.py:118
  18.0 6.9 convolution_convert_fusion
  38.6 22.4 %conditional.7 = (bf16[160,2048]{1,0:T(8,128)(2,1)}, bf16[160,2048]{1,0:T(8,128)(2,1)}, bf16[160,3072]{1,0:T(8,128)(2,1)S(1)}, bf16[160,1024]{1,0:T(8,128)(2,1)}, bf16[32,2048]{1,0:T(8,128)(2,1)}) conditional(s32[]{:T(128)} %convert_element_type.198, (bf16[160,2048]{1,0:T(8,128)(2,1)}, bf16[160,2048]{1,0:T(8,128)(2,1)}, ...), branch_computations={%region_2.2_spmd, %region_3.7_spmd} | conditional | flops 559183488 | bytes 21742856 | solution.py:118
  42.9 6.9 convolution_convert_fusion
  64.5 22.4 %conditional.7 = (bf16[160,2048]{1,0:T(8,128)(2,1)}, bf16[160,2048]{1,0:T(8,128)(2,1)}, bf16[160,3072]{1,0:T(8,128)(2,1)S(1)}, bf16[160,1024]{1,0:T(8,128)(2,1)}, bf16[32,2048]{1,0:T(8,128)(2,1)}) conditional(s32[]{:T(128)} %convert_element_type.198, (bf16[160,2048]{1,0:T(8,128)(2,1)}, bf16[160,2048]{1,0:T(8,128)(2,1)}, ...), branch_computations={%region_2.2_spmd, %region_3.7_spmd} | conditional | flops 559183488 | bytes 21742856 | solution.py:118
  68.7 6.9 convolution_convert_fusion
  91.0 22.4 %conditional.7 = (bf16[160,2048]{1,0:T(8,128)(2,1)}, bf16[160,2048]{1,0:T(8,128)(2,1)}, bf16[160,3072]{1,0:T(8,128)(2,1)S(1)}, bf16[160,1024]{1,0:T(8,128)(2,1)}, bf16[32,2048]{1,0:T(8,128)(2,1)}) conditional(s32[]{:T(128)} %convert_element_type.198, (bf16[160,2048]{1,0:T(8,128)(2,1)}, bf16[160,2048]{1,0:T(8,128)(2,1)}, ...), branch_computations={%region_2.2_spmd, %region_3.7_spmd} | conditional | flops 559183488 | bytes 21742856 | solution.py:118
  95.3 6.9 convolution_convert_fusion
  119.9 22.4 %conditional.7 = (bf16[160,2048]{1,0:T(8,128)(2,1)}, bf16[160,2048]{1,0:T(8,128)(2,1)}, bf16[160,3072]{1,0:T(8,128)(2,1)S(1)}, bf16[160,1024]{1,0:T(8,128)(2,1)}, bf16[32,2048]{1,0:T(8,128)(2,1)}) conditional(s32[]{:T(128)} %convert_element_type.198, (bf16[160,2048]{1,0:T(8,128)(2,1)}, bf16[160,2048]{1,0:T(8,128)(2,1)}, ...), branch_computations={%region_2.2_spmd, %region_3.7_spmd} | conditional | flops 559183488 | bytes 21742856 | solution.py:118
  124.1 6.9 convolution_convert_fusion
  148.8 22.4 %conditional.7 = (bf16[160,2048]{1,0:T(8,128)(2,1)}, bf16[160,2048]{1,0:T(8,128)(2,1)}, bf16[160,3072]{1,0:T(8,128)(2,1)S(1)}, bf16[160,1024]{1,0:T(8,128)(2,1)}, bf16[32,2048]{1,0:T(8,128)(2,1)}) conditional(s32[]{:T(128)} %convert_element_type.198, (bf16[160,2048]{1,0:T(8,128)(2,1)}, bf16[160,2048]{1,0:T(8,128)(2,1)}, ...), branch_computations={%region_2.2_spmd, %region_3.7_spmd} | conditional | flops 559183488 | bytes 21742856 | solution.py:118
  153.0 6.9 convolution_convert_fusion
  171.2 5.3 collective-permute-start
  177.7 22.4 %conditional.7 = (bf16[160,2048]{1,0:T(8,128)(2,1)}, bf16[160,2048]{1,0:T(8,128)(2,1)}, bf16[160,3072]{1,0:T(8,128)(2,1)S(1)}, bf16[160,1024]{1,0:T(8,128)(2,1)}, bf16[32,2048]{1,0:T(8,128)(2,1)}) conditional(s32[]{:T(128)} %convert_element_type.198, (bf16[160,2048]{1,0:T(8,128)(2,1)}, bf16[160,2048]{1,0:T(8,128)(2,1)}, ...), branch_computations={%region_2.2_spmd, %region_3.7_spmd} | conditional | flops 559183488 | bytes 21742856 | solution.py:118
  181.9 6.9 convolution_convert_fusion
  200.0 5.3 collective-permute-start
  206.5 22.4 %conditional.7 = (bf16[160,2048]{1,0:T(8,128)(2,1)}, bf16[160,2048]{1,0:T(8,128)(2,1)}, bf16[160,3072]{1,0:T(8,128)(2,1)S(1)}, bf16[160,1024]{1,0:T(8,128)(2,1)}, bf16[32,2048]{1,0:T(8,128)(2,1)}) conditional(s32[]{:T(128)} %convert_element_type.198, (bf16[160,2048]{1,0:T(8,128)(2,1)}, bf16[160,2048]{1,0:T(8,128)(2,1)}, ...), branch_computations={%region_2.2_spmd, %region_3.7_spmd} | conditional | flops 559183488 | bytes 21742856 | solution.py:118
  210.8 6.9 convolution_convert_fusion
  236.1 27.0 %collective-permute-start = (bf16[32,2048]{1,0:T(8,128)(2,1)}, bf16[32,2048]{1,0:T(8,128)(2,1)S(1)}, u32[]{:S(2)}, u32[]{:S(2)}) collective-permute-start(bf16[32,2048]{1,0:T(8,128)(2,1)} %get-tuple-element.1751), channel_id=1, source_target_pairs={{0,16},{16,32},{32,48},{48,64},{64,80},{80,96},{96,112},{1,17},{17... | collective-permute-start | bytes 393224 | tf_op jit(solution)/shard_map/while/body/eval_jaxpr/ppermute | solution.py:15
  272.1 27.0 %collective-permute-start = (bf16[32,2048]{1,0:T(8,128)(2,1)}, bf16[32,2048]{1,0:T(8,128)(2,1)S(1)}, u32[]{:S(2)}, u32[]{:S(2)}) collective-permute-start(bf16[32,2048]{1,0:T(8,128)(2,1)} %get-tuple-element.1751), channel_id=1, source_target_pairs={{0,16},{16,32},{32,48},{48,64},{64,80},{80,96},{96,112},{1,17},{17... | collective-permute-start | bytes 393224 | tf_op jit(solution)/shard_map/while/body/eval_jaxpr/ppermute | solution.py:15
  308.1 20.6 %collective-permute-start = (bf16[32,2048]{1,0:T(8,128)(2,1)}, bf16[32,2048]{1,0:T(8,128)(2,1)S(1)}, u32[]{:S(2)}, u32[]{:S(2)}) collective-permute-start(bf16[32,2048]{1,0:T(8,128)(2,1)} %get-tuple-element.1751), channel_id=1, source_target_pairs={{0,16},{16,32},{32,48},{48,64},{64,80},{80,96},{96,112},{1,17},{17... | collective-permute-start | bytes 393224 | tf_op jit(solution)/shard_map/while/body/eval_jaxpr/ppermute | solution.py:15
  337.7 24.7 %collective-permute-start = (bf16[32,2048]{1,0:T(8,128)(2,1)}, bf16[32,2048]{1,0:T(8,128)(2,1)S(1)}, u32[]{:S(2)}, u32[]{:S(2)}) collective-permute-start(bf16[32,2048]{1,0:T(8,128)(2,1)} %get-tuple-element.1751), channel_id=1, source_target_pairs={{0,16},{16,32},{32,48},{48,64},{64,80},{80,96},{96,112},{1,17},{17... | collective-permute-start | bytes 393224 | tf_op jit(solution)/shard_map/while/body/eval_jaxpr/ppermute | solution.py:15
  370.3 783.6 %while.53 = (s32[]{:T(128)}, bf16[32,2048]{1,0:T(8,128)(2,1)S(1)}, bf16[160,2048]{1,0:T(8,128)(2,1)}, bf16[160,3072]{1,0:T(8,128)(2,1)}, bf16[160,2048]{1,0:T(8,...) while((s32[]{:T(128)}, bf16[32,2048]{1,0:T(8,128)(2,1)S(1)}, ...), condition=%wide.region_20.21_spmd.clone.clone, body=%wide.region_10.20_spmd.clone.clone.sunk | while | flops 593570176 | bytes 31797260 | solution.py:236
  379.3 21.1 %collective-permute-done.1 = bf16[32,2048]{1,0:T(8,128)(2,1)S(1)} collective-permute-done((bf16[32,2048]{1,0:T(8,128)(2,1)}, bf16[32,2048]{1,0:T(8,128)(2,1)S(1)}, u32[]{:S(2)}, u32[]{:S(2)}) %collective-permute-start.1) | collective-permute-done | bytes 131104 | tf_op jit(solution)/shard_map/while/body/eval_jaxpr/ppermute | solution.py:15
  409.5 25.1 %collective-permute-done.1 = bf16[32,2048]{1,0:T(8,128)(2,1)S(1)} collective-permute-done((bf16[32,2048]{1,0:T(8,128)(2,1)}, bf16[32,2048]{1,0:T(8,128)(2,1)S(1)}, u32[]{:S(2)}, u32[]{:S(2)}) %collective-permute-start.1) | collective-permute-done | bytes 131104 | tf_op jit(solution)/shard_map/while/body/eval_jaxpr/ppermute | solution.py:15
  443.7 20.9 %collective-permute-done.1 = bf16[32,2048]{1,0:T(8,128)(2,1)S(1)} collective-permute-done((bf16[32,2048]{1,0:T(8,128)(2,1)}, bf16[32,2048]{1,0:T(8,128)(2,1)S(1)}, u32[]{:S(2)}, u32[]{:S(2)}) %collective-permute-start.1) | collective-permute-done | bytes 131104 | tf_op jit(solution)/shard_map/while/body/eval_jaxpr/ppermute | solution.py:15
  466.6 296.2 %collective-permute-done.1 = bf16[32,2048]{1,0:T(8,128)(2,1)S(1)} collective-permute-done((bf16[32,2048]{1,0:T(8,128)(2,1)}, bf16[32,2048]{1,0:T(8,128)(2,1)S(1)}, u32[]{:S(2)}, u32[]{:S(2)}) %collective-permute-start.1) | collective-permute-done | bytes 131104 | tf_op jit(solution)/shard_map/while/body/eval_jaxpr/ppermute | solution.py:15
  762.8 42.8 %conditional.8 = (bf16[160,2048]{1,0:T(8,128)(2,1)}, bf16[160,3072]{1,0:T(8,128)(2,1)}, bf16[160,2048]{1,0:T(8,128)(2,1)}, bf16[160,2048]{1,0:T(8,128)(2,1)}, f3...) conditional(s32[]{:T(128)} %convert_element_type.199, ...), branch_computations={%region_11.11_spmd, %region_12.19_spmd.clone} | conditional | flops 593570176 | bytes 31271688 | solution.py:218
  787.9 8.5 fusion.76
  812.1 42.8 %conditional.8 = (bf16[160,2048]{1,0:T(8,128)(2,1)}, bf16[160,3072]{1,0:T(8,128)(2,1)}, bf16[160,2048]{1,0:T(8,128)(2,1)}, bf16[160,2048]{1,0:T(8,128)(2,1)}, f3...) conditional(s32[]{:T(128)} %convert_element_type.199, ...), branch_computations={%region_11.11_spmd, %region_12.19_spmd.clone} | conditional | flops 593570176 | bytes 31271688 | solution.py:218
  837.1 8.5 fusion.76
  861.4 42.8 %conditional.8 = (bf16[160,2048]{1,0:T(8,128)(2,1)}, bf16[160,3072]{1,0:T(8,128)(2,1)}, bf16[160,2048]{1,0:T(8,128)(2,1)}, bf16[160,2048]{1,0:T(8,128)(2,1)}, f3...) conditional(s32[]{:T(128)} %convert_element_type.199, ...), branch_computations={%region_11.11_spmd, %region_12.19_spmd.clone} | conditional | flops 593570176 | bytes 31271688 | solution.py:218
  886.4 8.5 fusion.76
  910.7 42.8 %conditional.8 = (bf16[160,2048]{1,0:T(8,128)(2,1)}, bf16[160,3072]{1,0:T(8,128)(2,1)}, bf16[160,2048]{1,0:T(8,128)(2,1)}, bf16[160,2048]{1,0:T(8,128)(2,1)}, f3...) conditional(s32[]{:T(128)} %convert_element_type.199, ...), branch_computations={%region_11.11_spmd, %region_12.19_spmd.clone} | conditional | flops 593570176 | bytes 31271688 | solution.py:218
  935.7 8.5 fusion.76
  959.9 42.8 %conditional.8 = (bf16[160,2048]{1,0:T(8,128)(2,1)}, bf16[160,3072]{1,0:T(8,128)(2,1)}, bf16[160,2048]{1,0:T(8,128)(2,1)}, bf16[160,2048]{1,0:T(8,128)(2,1)}, f3...) conditional(s32[]{:T(128)} %convert_element_type.199, ...), branch_computations={%region_11.11_spmd, %region_12.19_spmd.clone} | conditional | flops 593570176 | bytes 31271688 | solution.py:218
  985.0 8.5 fusion.76
  1009.2 42.8 %conditional.8 = (bf16[160,2048]{1,0:T(8,128)(2,1)}, bf16[160,3072]{1,0:T(8,128)(2,1)}, bf16[160,2048]{1,0:T(8,128)(2,1)}, bf16[160,2048]{1,0:T(8,128)(2,1)}, f3...) conditional(s32[]{:T(128)} %convert_element_type.199, ...), branch_computations={%region_11.11_spmd, %region_12.19_spmd.clone} | conditional | flops 593570176 | bytes 31271688 | solution.py:218
  1034.2 8.5 fusion.76
  1058.5 42.8 %conditional.8 = (bf16[160,2048]{1,0:T(8,128)(2,1)}, bf16[160,3072]{1,0:T(8,128)(2,1)}, bf16[160,2048]{1,0:T(8,128)(2,1)}, bf16[160,2048]{1,0:T(8,128)(2,1)}, f3...) conditional(s32[]{:T(128)} %convert_element_type.199, ...), branch_computations={%region_11.11_spmd, %region_12.19_spmd.clone} | conditional | flops 593570176 | bytes 31271688 | solution.py:218
  1083.5 8.5 fusion.76
  1107.7 42.8 %conditional.8 = (bf16[160,2048]{1,0:T(8,128)(2,1)}, bf16[160,3072]{1,0:T(8,128)(2,1)}, bf16[160,2048]{1,0:T(8,128)(2,1)}, bf16[160,2048]{1,0:T(8,128)(2,1)}, f3...) conditional(s32[]{:T(128)} %convert_element_type.199, ...), branch_computations={%region_11.11_spmd, %region_12.19_spmd.clone} | conditional | flops 593570176 | bytes 31271688 | solution.py:218
  1132.7 8.5 fusion.76
  1158.3 6.4 copy.56
  1164.8 7.5 multiply_convert_fusion.2
  1174.6 67.6 %reduce-scatter.7.cloned.1.call-done = bf16[128,1024]{1,0:T(8,128)(2,1)} async-done(((bf16[2048,1024]{1,0:T(8,128)(2,1)}), bf16[128,1024]{1,0:T(8,128)(2,1)}) %reduce-scatter.7.cloned.1.call-update) | async-done | bytes 262160
  1244.1 96.3 %reduce-scatter.5.cloned.1.call-done = bf16[128,3072]{1,0:T(8,128)(2,1)} async-done(((bf16[2048,3072]{1,0:T(8,128)(2,1)}), bf16[128,3072]{1,0:T(8,128)(2,1)}) %reduce-scatter.5.cloned.1.call-update) | async-done | bytes 786448 | tf_op jit(solution)/shard_map/reduce_scatter | solution.py:247
  (638 shorter events, 535.2 us)
Async XLA Ops:
  7.2 1235.1 %reduce-scatter.7.cloned.1.call-start = ((), (), s32[]{:S(2)}) async-start(), calls=%async_computation.3 | async-start | bytes 4456448
  36.2 2.5 collective-permute-start
  61.0 3.4 collective-permute-start
  86.9 4.2 collective-permute-start
  113.4 6.5 collective-permute-start
  142.3 6.5 collective-permute-start
  171.2 6.5 collective-permute-start
  200.0 6.5 collective-permute-start
  228.9 6.5 collective-permute-start
  236.1 28.2 %collective-permute-start = (bf16[32,2048]{1,0:T(8,128)(2,1)}, bf16[32,2048]{1,0:T(8,128)(2,1)S(1)}, u32[]{:S(2)}, u32[]{:S(2)}) collective-permute-start(bf16[32,2048]{1,0:T(8,128)(2,1)} %get-tuple-element.1751), channel_id=1, source_target_pairs={{0,16},{16,32},{32,48},{48,64},{64,80},{80,96},{96,112},{1,17},{17... | collective-permute-start | bytes 393224 | tf_op jit(solution)/shard_map/while/body/eval_jaxpr/ppermute | solution.py:15
  265.0 6.5 collective-permute-start
  272.1 28.2 %collective-permute-start = (bf16[32,2048]{1,0:T(8,128)(2,1)}, bf16[32,2048]{1,0:T(8,128)(2,1)S(1)}, u32[]{:S(2)}, u32[]{:S(2)}) collective-permute-start(bf16[32,2048]{1,0:T(8,128)(2,1)} %get-tuple-element.1751), channel_id=1, source_target_pairs={{0,16},{16,32},{32,48},{48,64},{64,80},{80,96},{96,112},{1,17},{17... | collective-permute-start | bytes 393224 | tf_op jit(solution)/shard_map/while/body/eval_jaxpr/ppermute | solution.py:15
  301.0 6.5 collective-permute-start
  308.1 21.8 %collective-permute-start = (bf16[32,2048]{1,0:T(8,128)(2,1)}, bf16[32,2048]{1,0:T(8,128)(2,1)S(1)}, u32[]{:S(2)}, u32[]{:S(2)}) collective-permute-start(bf16[32,2048]{1,0:T(8,128)(2,1)} %get-tuple-element.1751), channel_id=1, source_target_pairs={{0,16},{16,32},{32,48},{48,64},{64,80},{80,96},{96,112},{1,17},{17... | collective-permute-start | bytes 393224 | tf_op jit(solution)/shard_map/while/body/eval_jaxpr/ppermute | solution.py:15
  330.6 6.5 collective-permute-start
  337.7 25.9 %collective-permute-start = (bf16[32,2048]{1,0:T(8,128)(2,1)}, bf16[32,2048]{1,0:T(8,128)(2,1)S(1)}, u32[]{:S(2)}, u32[]{:S(2)}) collective-permute-start(bf16[32,2048]{1,0:T(8,128)(2,1)} %get-tuple-element.1751), channel_id=1, source_target_pairs={{0,16},{16,32},{32,48},{48,64},{64,80},{80,96},{96,112},{1,17},{17... | collective-permute-start | bytes 393224 | tf_op jit(solution)/shard_map/while/body/eval_jaxpr/ppermute | solution.py:15
  371.0 6.3 collective-permute-start.1
  378.0 22.4 %collective-permute-start.1 = (bf16[32,2048]{1,0:T(8,128)(2,1)}, bf16[32,2048]{1,0:T(8,128)(2,1)S(1)}, u32[]{:S(2)}, u32[]{:S(2)}) collective-permute-start(bf16[32,2048]{1,0:T(8,128)(2,1)} %get-tuple-element.1776), channel_id=1, source_target_pairs={{16,0},{32,16},{48,32},{64,48},{80,64},{96,80},{112,96},{17,1},{33... | collective-permute-start | bytes 393224 | tf_op jit(solution)/shard_map/while/body/eval_jaxpr/ppermute | solution.py:15
  401.1 6.5 collective-permute-start.1
  408.2 26.4 %collective-permute-start.1 = (bf16[32,2048]{1,0:T(8,128)(2,1)}, bf16[32,2048]{1,0:T(8,128)(2,1)S(1)}, u32[]{:S(2)}, u32[]{:S(2)}) collective-permute-start(bf16[32,2048]{1,0:T(8,128)(2,1)} %get-tuple-element.1776), channel_id=1, source_target_pairs={{16,0},{32,16},{48,32},{64,48},{80,64},{96,80},{112,96},{17,1},{33... | collective-permute-start | bytes 393224 | tf_op jit(solution)/shard_map/while/body/eval_jaxpr/ppermute | solution.py:15
  435.3 6.5 collective-permute-start.1
  442.4 22.2 %collective-permute-start.1 = (bf16[32,2048]{1,0:T(8,128)(2,1)}, bf16[32,2048]{1,0:T(8,128)(2,1)S(1)}, u32[]{:S(2)}, u32[]{:S(2)}) collective-permute-start(bf16[32,2048]{1,0:T(8,128)(2,1)} %get-tuple-element.1776), channel_id=1, source_target_pairs={{16,0},{32,16},{48,32},{64,48},{80,64},{96,80},{112,96},{17,1},{33... | collective-permute-start | bytes 393224 | tf_op jit(solution)/shard_map/while/body/eval_jaxpr/ppermute | solution.py:15
  465.3 297.5 %collective-permute-start.1 = (bf16[32,2048]{1,0:T(8,128)(2,1)}, bf16[32,2048]{1,0:T(8,128)(2,1)S(1)}, u32[]{:S(2)}, u32[]{:S(2)}) collective-permute-start(bf16[32,2048]{1,0:T(8,128)(2,1)} %get-tuple-element.1776), channel_id=1, source_target_pairs={{16,0},{32,16},{48,32},{64,48},{80,64},{96,80},{112,96},{17,1},{33... | collective-permute-start | bytes 393224 | tf_op jit(solution)/shard_map/while/body/eval_jaxpr/ppermute | solution.py:15
  785.3 11.1 copy-start.5
  786.7 13.5 %copy-start.1 = (bf16[32,2048]{1,0:T(8,128)(2,1)S(1)}, bf16[32,2048]{1,0:T(8,128)(2,1)}, u32[]{:S(2)}) copy-start(bf16[32,2048]{1,0:T(8,128)(2,1)} %get-tuple-element.1547) | copy-start | bytes 393220 | tf_op jit(solution)/shard_map/while/body/eval_jaxpr/cond
  805.6 6.5 collective-permute-start.1
  834.6 11.1 copy-start.5
  836.0 13.5 %copy-start.1 = (bf16[32,2048]{1,0:T(8,128)(2,1)S(1)}, bf16[32,2048]{1,0:T(8,128)(2,1)}, u32[]{:S(2)}) copy-start(bf16[32,2048]{1,0:T(8,128)(2,1)} %get-tuple-element.1547) | copy-start | bytes 393220 | tf_op jit(solution)/shard_map/while/body/eval_jaxpr/cond
  854.9 6.5 collective-permute-start.1
  883.8 11.1 copy-start.5
  885.2 13.5 %copy-start.1 = (bf16[32,2048]{1,0:T(8,128)(2,1)S(1)}, bf16[32,2048]{1,0:T(8,128)(2,1)}, u32[]{:S(2)}) copy-start(bf16[32,2048]{1,0:T(8,128)(2,1)} %get-tuple-element.1547) | copy-start | bytes 393220 | tf_op jit(solution)/shard_map/while/body/eval_jaxpr/cond
  904.1 6.5 collective-permute-start.1
  933.1 11.1 copy-start.5
  934.5 13.5 %copy-start.1 = (bf16[32,2048]{1,0:T(8,128)(2,1)S(1)}, bf16[32,2048]{1,0:T(8,128)(2,1)}, u32[]{:S(2)}) copy-start(bf16[32,2048]{1,0:T(8,128)(2,1)} %get-tuple-element.1547) | copy-start | bytes 393220 | tf_op jit(solution)/shard_map/while/body/eval_jaxpr/cond
  953.5 6.5 collective-permute-start.1
  982.4 11.1 copy-start.5
  983.8 13.5 %copy-start.1 = (bf16[32,2048]{1,0:T(8,128)(2,1)S(1)}, bf16[32,2048]{1,0:T(8,128)(2,1)}, u32[]{:S(2)}) copy-start(bf16[32,2048]{1,0:T(8,128)(2,1)} %get-tuple-element.1547) | copy-start | bytes 393220 | tf_op jit(solution)/shard_map/while/body/eval_jaxpr/cond
  1002.7 6.5 collective-permute-start.1
  1031.7 11.1 copy-start.5
  1033.1 13.5 %copy-start.1 = (bf16[32,2048]{1,0:T(8,128)(2,1)S(1)}, bf16[32,2048]{1,0:T(8,128)(2,1)}, u32[]{:S(2)}) copy-start(bf16[32,2048]{1,0:T(8,128)(2,1)} %get-tuple-element.1547) | copy-start | bytes 393220 | tf_op jit(solution)/shard_map/while/body/eval_jaxpr/cond
  1052.0 6.5 collective-permute-start.1
  1080.9 11.1 copy-start.5
  1082.3 13.5 %copy-start.1 = (bf16[32,2048]{1,0:T(8,128)(2,1)S(1)}, bf16[32,2048]{1,0:T(8,128)(2,1)}, u32[]{:S(2)}) copy-start(bf16[32,2048]{1,0:T(8,128)(2,1)} %get-tuple-element.1547) | copy-start | bytes 393220 | tf_op jit(solution)/shard_map/while/body/eval_jaxpr/cond
  1101.2 6.5 collective-permute-start.1
  1130.2 11.1 copy-start.5
  1131.6 13.5 %copy-start.1 = (bf16[32,2048]{1,0:T(8,128)(2,1)S(1)}, bf16[32,2048]{1,0:T(8,128)(2,1)}, u32[]{:S(2)}) copy-start(bf16[32,2048]{1,0:T(8,128)(2,1)} %get-tuple-element.1547) | copy-start | bytes 393220 | tf_op jit(solution)/shard_map/while/body/eval_jaxpr/cond
  1150.5 3.4 collective-permute-start.1
  1164.7 175.7 %reduce-scatter.5.cloned.1.call-start = ((), (), s32[]{:S(2)}) async-start(), calls=%async_computation.2 | async-start | bytes 13369344 | tf_op jit(solution)/shard_map/reduce_scatter | solution.py:247
  (25 other events, 154.0 us)
Sparse Core Ops, SparseCore 0:
  1164.9 77.3 reduce-scatter.6
  1246.7 93.6 reduce-scatter.4
where the time goes:
time: 1350 us
  waiting for transfers between devices  599 us (44%)
  matrix products  237 us (18%)
  local copies, waits for them, and re-layouts  181 us (13%)
  starting transfers between devices  168 us (12%)
  other arithmetic  115 us (9%)
  loops' own time  33.1 us (2%)
  between operations  14.1 us (1%)
    ppermute x30, waiting for transfers between devices, shifted_2(): return lax.ppermute(shard, axis, pairs)  435 us
    ppermute x30, starting transfers between devices, shifted_2(): return lax.ppermute(shard, axis, pairs)  168 us
    reduce_scatter x1, waiting for transfers between devices, on_device(): lax.psum_scatter(term_in.astype(jnp.bfloat16), 'dp', scatter_dimension=0,...  96.3 us
    dot_general x16, matrix products, contract_cols(): lax.dot_general(left, right, (((1,), (1,)), ((), ())), preferred_element_...  96.1 us
    unnamed x3, waiting for transfers between devices  67.7 us
    dynamic_update_slice x32, local copies, waits for them, and re-layouts, place(): lax.dynamic_update_slice_in_dim(buffer, jnp.where(live_rows, new_rows, pr...  57.4 us
    dot_general x8, matrix products, forward_compute_block(): jnp.dot(normed, weight_in, preferred_element_type=jnp.float32)  55 us
    select_n x24, other arithmetic, place(): jnp.where(live_rows, new_rows, previous)  39 us
  transfers between devices with their start and end apart: 32, of which 32 were waited for; matrix products, arithmetic and copies ran while one was open for 1% of the time, Pallas kernels for 0%

commit v1 on v0

v1 whole, which is shorter than its diff:
```python
import math

import jax
import jax.numpy as jnp
from jax import lax
from jax.experimental import pallas as pl
from jax.experimental.pallas import tpu as pltpu
from jax.sharding import PartitionSpec as P

HS = 128
CHUNKS = 1
SUB = 16
MESH = pl.DeviceIdType.MESH
F32 = jnp.float32
BF16 = jnp.bfloat16


def kernel(
    lens,
    tok,
    cot,
    win,
    wout,
    so,
    ig,
    gi,
    go,
    w_in,
    w_out,
    w_in_t,
    w_out_t,
    x_in,
    x_hat,
    inv_std,
    normed,
    proj,
    probs,
    mixed,
    out,
    up,
    grad_mixed,
    key_acc,
    val_acc,
    gp,
    gn,
    gin,
    n_t,
    m_t,
    n_g,
    m_g,
    gp_g,
    up_g,
    part,
    go_buf,
    win_sem,
    wout_sem,
    local_sem,
    own_sem,
    fwd_send,
    fwd_recv,
    bwd_send,
    bwd_recv,
    n_send,
    n_recv,
    m_send,
    m_recv,
    gp_send,
    gp_recv,
    up_send,
    up_recv,
    fin_send,
    fin_recv,
):
    sections = 8
    n_dp = 16
    side = 4
    sec = lax.axis_index("section")
    me = lax.axis_index("dp")
    my_z, my_x = me // side, lax.rem(me, side)
    seq, width = x_in.shape
    inner = w_out.shape[0]
    heads = inner // HS
    rows_c = seq // CHUNKS
    n_rows = width // side
    gp_cols = 3 * inner // side
    up_cols = width // n_dp
    w_blk = win_sem.shape[0]
    w_cols = 3 * inner // w_blk
    scale = 1.0 / math.sqrt(HS)
    grad_scale = 1.0 / math.sqrt(seq * n_dp)

    def win_copy(j):
        cols = pl.ds(j * w_cols, w_cols)
        return pltpu.make_async_copy(win.at[0, :, cols], w_in.at[:, cols], win_sem.at[j])

    wout_copy = pltpu.make_async_copy(wout.at[0], w_out, wout_sem)
    tok_copy = pltpu.make_async_copy(tok, x_in, local_sem.at[0])
    cot_copy = pltpu.make_async_copy(cot, up, local_sem.at[1])

    @pl.when(sec == 0)
    def _():
        tok_copy.start()

    @pl.when(sec == sections - 1)
    def _():
        cot_copy.start()

    for j in range(w_blk):
        win_copy(j).start()
    wout_copy.start()

    barrier = pltpu.get_barrier_semaphore()

    def greet(d, _):
        pl.semaphore_signal(
            barrier, inc=1, device_id={"dp": lax.rem(me + d, n_dp)}, device_id_type=MESH
        )
        return 0

    lax.fori_loop(1, n_dp, greet, 0)
    for step in (1, sections - 1):
        pl.semaphore_signal(
            barrier,
            inc=1,
            device_id={"section": lax.rem(sec + step, sections)},
            device_id_type=MESH,
        )
    pl.semaphore_wait(barrier, n_dp + 1)

    row_at = lax.broadcasted_iota(jnp.int32, (seq, seq), 0)
    col_at = lax.broadcasted_iota(jnp.int32, (seq, seq), 1)
    row_slice = jnp.zeros((seq, seq), jnp.int32)
    col_slice = jnp.zeros((seq, seq), jnp.int32)
    end = jnp.int32(0)
    for j in range(lens.shape[1]):
        end = end + lens[0, j]
        row_slice = row_slice + jnp.where(row_at >= end, 1, 0)
        col_slice = col_slice + jnp.where(col_at >= end, 1, 0)
    same = row_slice == col_slice
    causal = col_at <= row_at
    if CHUNKS > 1:
        proj[...] = jnp.zeros_like(proj)

    def transpose_weights():
        blk = 512

        def turn(source, dest):
            rows, cols = source.shape
            wide = cols // blk

            def one(i, _):
                r = pl.multiple_of((i // wide) * blk, blk)
                c = pl.multiple_of(lax.rem(i, wide) * blk, blk)
                dest[pl.ds(c, blk), pl.ds(r, blk)] = source[pl.ds(r, blk), pl.ds(c, blk)].T
                return 0

            lax.fori_loop(0, (rows // blk) * wide, one, 0)

        turn(w_in, w_in_t)
        turn(w_out, w_out_t)

    @pl.when(sec > 0)
    def _():
        for j in range(w_blk):
            win_copy(j).wait()
        wout_copy.wait()

    @pl.when(sec >= sections // 2)
    def _():
        transpose_weights()

    def fwd_hop(c):
        rows = pl.ds(c * rows_c, rows_c)
        return pltpu.make_async_remote_copy(
            src_ref=out.at[rows],
            dst_ref=x_in.at[rows],
            send_sem=fwd_send.at[c],
            recv_sem=fwd_recv.at[c],
            device_id={"section": lax.rem(sec + 1, sections)},
            device_id_type=MESH,
        )

    def so_copy(c):
        rows = pl.ds(c * rows_c, rows_c)
        return pltpu.make_async_copy(out.at[rows], so.at[0, rows], local_sem.at[2 + c])

    @pl.when(sec == 0)
    def _():
        tok_copy.wait()

    for c in range(CHUNKS):
        r0 = c * rows_c
        rows = slice(r0, r0 + rows_c)

        @pl.when(sec > 0)
        def _():
            fwd_hop(c).wait_recv()

        for r in range(r0, r0 + rows_c, SUB):
            sub = slice(r, r + SUB)
            values = x_in[sub, :].astype(F32)
            centre = jnp.mean(values, -1, keepdims=True)
            shifted = values - centre
            inv = lax.rsqrt(jnp.mean(shifted * shifted, -1, keepdims=True) + 1e-05)
            hat = shifted * inv
            x_hat[sub, :] = hat
            inv_std[sub, :] = jnp.broadcast_to(inv, (SUB, 128))
            normed[sub, :] = hat.astype(BF16)

        for j in range(w_blk):
            if c == 0:

                @pl.when(sec == 0)
                def _():
                    win_copy(j).wait()

            cols = slice(j * w_cols, (j + 1) * w_cols)
            proj[rows, cols] = jnp.dot(
                normed[rows, :], w_in[:, cols], preferred_element_type=F32
            ).astype(BF16)

        for h in range(heads):
            q = proj[rows, h * HS : (h + 1) * HS]
            k = proj[:, inner + h * HS : inner + (h + 1) * HS]
            v = proj[:, 2 * inner + h * HS : 2 * inner + (h + 1) * HS]
            scores = (
                lax.dot_general(q, k, (((1,), (1,)), ((), ())), preferred_element_type=F32) * scale
            )
            scores = jnp.where(causal[rows, :], scores, -jnp.inf)
            top = jnp.max(scores, -1, keepdims=True)
            weight = jnp.exp(scores - top)
            p = weight / jnp.sum(weight, -1, keepdims=True)
            probs[h, rows, :] = p
            mixed[rows, h * HS : (h + 1) * HS] = jnp.dot(
                p.astype(BF16), v, preferred_element_type=F32
            ).astype(BF16)

        if c == 0:

            @pl.when(sec == 0)
            def _():
                wout_copy.wait()

        for j in range(0, width, 512):
            cols = slice(j, j + 512)
            out[rows, cols] = (
                x_in[rows, cols].astype(F32)
                + jnp.dot(mixed[rows, :], w_out[:, cols], preferred_element_type=F32)
            ).astype(BF16)

        @pl.when(sec < sections - 1)
        def _():
            fwd_hop(c).start()

        so_copy(c).start()

    def partner(d):
        to = lax.rem(me + d, n_dp)
        return to, to // side, lax.rem(to, side)

    mine = pl.ds(pl.multiple_of(me * seq, seq), seq)

    def n_copy(d):
        to, z, _ = partner(d)
        return pltpu.make_async_remote_copy(
            src_ref=n_t.at[pl.ds(pl.multiple_of(z * n_rows, n_rows), n_rows)],
            dst_ref=n_g.at[:, mine],
            send_sem=n_send.at[d],
            recv_sem=n_recv.at[d],
            device_id={"dp": to},
            device_id_type=MESH,
        )

    def m_copy(d):
        to, _, _ = partner(d)
        return pltpu.make_async_remote_copy(
            src_ref=m_t,
            dst_ref=m_g.at[:, mine],
            send_sem=m_send.at[d],
            recv_sem=m_recv.at[d],
            device_id={"dp": to},
            device_id_type=MESH,
        )

    def up_copy(d):
        to, _, _ = partner(d)
        return pltpu.make_async_remote_copy(
            src_ref=up.at[:, pl.ds(pl.multiple_of(to * up_cols, up_cols), up_cols)],
            dst_ref=up_g.at[mine],
            send_sem=up_send.at[d],
            recv_sem=up_recv.at[d],
            device_id={"dp": to},
            device_id_type=MESH,
        )

    def gp_copy(c, d):
        to, _, x = partner(d)
        return pltpu.make_async_remote_copy(
            src_ref=gp.at[
                pl.ds(c * rows_c, rows_c), pl.ds(pl.multiple_of(x * gp_cols, gp_cols), gp_cols)
            ],
            dst_ref=gp_g.at[pl.ds(pl.multiple_of(me * seq + c * rows_c, rows_c), rows_c)],
            send_sem=gp_send.at[c, d],
            recv_sem=gp_recv.at[c, d],
            device_id={"dp": to},
            device_id_type=MESH,
        )

    n_own = pltpu.make_async_copy(
        n_t.at[pl.ds(pl.multiple_of(my_z * n_rows, n_rows), n_rows)], n_g.at[:, mine], own_sem.at[0]
    )
    m_own = pltpu.make_async_copy(m_t, m_g.at[:, mine], own_sem.at[1])
    up_own = pltpu.make_async_copy(
        up.at[:, pl.ds(pl.multiple_of(me * up_cols, up_cols), up_cols)],
        up_g.at[mine],
        own_sem.at[2],
    )
    gp_own = pltpu.make_async_copy(
        gp.at[:, pl.ds(pl.multiple_of(my_x * gp_cols, gp_cols), gp_cols)],
        gp_g.at[mine],
        own_sem.at[3],
    )

    def each(start, *fns):
        def one(d, _):
            for fn in fns:
                fn(d)
            return 0

        lax.fori_loop(1, n_dp, one, 0)

    for r in range(0, width, 512):
        n_t[r : r + 512, :] = normed[:, r : r + 512].T
    for r in range(0, inner, 512):
        m_t[r : r + 512, :] = mixed[:, r : r + 512].T
    each(None, lambda d: n_copy(d).start(), lambda d: m_copy(d).start())
    n_own.start()
    m_own.start()

    @pl.when(sec < sections // 2)
    def _():
        transpose_weights()

    def bwd_hop(c):
        rows = pl.ds(c * rows_c, rows_c)
        return pltpu.make_async_remote_copy(
            src_ref=gin.at[rows],
            dst_ref=up.at[rows],
            send_sem=bwd_send.at[c],
            recv_sem=bwd_recv.at[c],
            device_id={"section": lax.rem(sec + sections - 1, sections)},
            device_id_type=MESH,
        )

    def ig_copy(c):
        rows = pl.ds(c * rows_c, rows_c)
        return pltpu.make_async_copy(gin.at[rows], ig.at[0, rows], local_sem.at[2 + CHUNKS + c])

    @pl.when(sec == sections - 1)
    def _():
        cot_copy.wait()

    for c in reversed(range(CHUNKS)):
        r0 = c * rows_c
        rows = slice(r0, r0 + rows_c)

        @pl.when(sec < sections - 1)
        def _():
            bwd_hop(c).wait_recv()

        for j in range(0, inner, 512):
            cols = slice(j, j + 512)
            grad_mixed[rows, cols] = jnp.dot(
                up[rows, :], w_out_t[:, cols], preferred_element_type=F32
            ).astype(BF16)

        for h in range(heads):
            at = slice(h * HS, (h + 1) * HS)
            k_at = slice(inner + h * HS, inner + (h + 1) * HS)
            v_at = slice(2 * inner + h * HS, 2 * inner + (h + 1) * HS)
            q, k, v = proj[rows, at], proj[:, k_at], proj[:, v_at]
            g = grad_mixed[rows, at]
            p = probs[h, rows, :]
            grad_p = lax.dot_general(g, v, (((1,), (1,)), ((), ())), preferred_element_type=F32)
            delta = jnp.sum(p * grad_p, -1, keepdims=True)
            grad_s = p * (grad_p - delta)
            gp[rows, at] = (
                jnp.dot(grad_s.astype(BF16), k, preferred_element_type=F32) * scale
            ).astype(BF16)
            live = same[rows, :]
            grad_s = jnp.where(live, grad_s, 0.0).astype(BF16)
            p = jnp.where(live, p, 0.0).astype(BF16)
            gk = lax.dot_general(grad_s, q, (((0,), (0,)), ((), ())), preferred_element_type=F32)
            gv = lax.dot_general(p, g, (((0,), (0,)), ((), ())), preferred_element_type=F32)
            if c < CHUNKS - 1:
                gk = gk + key_acc[:, at]
                gv = gv + val_acc[:, at]
            if c > 0:
                key_acc[:, at] = gk
                val_acc[:, at] = gv
            gp[rows, k_at] = (gk[rows, :] * scale).astype(BF16)
            gp[rows, v_at] = gv[rows, :].astype(BF16)

        @pl.when(sec == 0)
        def _():
            each(None, lambda d: gp_copy(c, d).start())

        for j in range(0, width, 512):
            cols = slice(j, j + 512)
            gn[rows, cols] = jnp.dot(gp[rows, :], w_in_t[:, cols], preferred_element_type=F32)

        for r in range(r0, r0 + rows_c, SUB):
            sub = slice(r, r + SUB)
            g = gn[sub, :]
            hat = x_hat[sub, :]
            mean_g = jnp.mean(g, -1, keepdims=True)
            mean_gh = jnp.mean(g * hat, -1, keepdims=True)
            grad = inv_std[sub, :1] * (g - mean_g - hat * mean_gh)
            gin[sub, :] = (up[sub, :].astype(F32) + grad).astype(BF16)

        @pl.when(sec > 0)
        def _():
            bwd_hop(c).start()
            each(None, lambda d: gp_copy(c, d).start())

        ig_copy(c).start()

    each(None, lambda d: up_copy(d).start())
    up_own.start()
    gp_own.start()

    m_own.wait()
    up_own.wait()
    each(None, lambda d: m_copy(d).wait_recv(), lambda d: up_copy(d).wait_recv())
    for r in range(0, inner, 256):
        go_buf[r : r + 256, :] = (
            jnp.dot(m_g[r : r + 256, :], up_g[...], preferred_element_type=F32) * grad_scale
        ).astype(BF16)
    go_copy = pltpu.make_async_copy(go_buf, go.at[0], local_sem.at[2 + 2 * CHUNKS])
    go_copy.start()

    n_own.wait()
    gp_own.wait()
    each(
        None,
        lambda d: n_copy(d).wait_recv(),
        *[lambda d, c=c: gp_copy(c, d).wait_recv() for c in range(CHUNKS)],
    )

    def fin_copy(d):
        x = lax.rem(my_x + d, side)
        return pltpu.make_async_remote_copy(
            src_ref=part.at[d],
            dst_ref=gi.at[0, :, pl.ds(pl.multiple_of(my_x * gp_cols, gp_cols), gp_cols)],
            send_sem=fin_send.at[d],
            recv_sem=fin_recv.at[d],
            device_id={"dp": my_z * side + x},
            device_id_type=MESH,
        )

    fin_own = pltpu.make_async_copy(
        part.at[0],
        gi.at[0, :, pl.ds(pl.multiple_of(my_x * gp_cols, gp_cols), gp_cols)],
        own_sem.at[4],
    )
    for d in (2, 1, 3, 0):
        x = lax.rem(my_x + d, side)
        part[d] = (
            jnp.dot(
                n_g[pl.ds(pl.multiple_of(x * seq, seq), seq), :],
                gp_g[...],
                preferred_element_type=F32,
            )
            * grad_scale
        ).astype(BF16)
        if d:
            fin_copy(d).start()
        else:
            fin_own.start()

    each(
        None,
        lambda d: n_copy(d).wait_send(),
        lambda d: m_copy(d).wait_send(),
        lambda d: up_copy(d).wait_send(),
        *[lambda d, c=c: gp_copy(c, d).wait_send() for c in range(CHUNKS)],
    )
    for c in range(CHUNKS):

        @pl.when(sec < sections - 1)
        def _():
            fwd_hop(c).wait_send()

        @pl.when(sec > 0)
        def _():
            bwd_hop(c).wait_send()

        so_copy(c).wait()
        ig_copy(c).wait()
    go_copy.wait()
    fin_own.wait()
    for d in (1, 2, 3):
        fin_copy(d).wait()


def on_device(tokens_in, cotangent, in_weights, out_weights, slice_lengths):
    seq, width = tokens_in.shape
    inner = out_weights.shape[1]
    heads = inner // HS
    n_dp, side = 16, 4
    any_space = pl.BlockSpec(memory_space=pl.ANY)
    vmem = pltpu.VMEM
    dma = pltpu.SemaphoreType.DMA
    w_blk = 4
    scratch = [
        vmem((width, 3 * inner), BF16),
        vmem((inner, width), BF16),
        vmem((3 * inner, width), BF16),
        vmem((width, inner), BF16),
        vmem((seq, width), BF16),
        vmem((seq, width), F32),
        vmem((seq, 128), F32),
        vmem((seq, width), BF16),
        vmem((seq, 3 * inner), BF16),
        vmem((heads, seq, seq), F32),
        vmem((seq, inner), BF16),
        vmem((seq, width), BF16),
        vmem((seq, width), BF16),
        vmem((seq, inner), BF16),
        vmem((seq, inner), F32),
        vmem((seq, inner), F32),
        vmem((seq, 3 * inner), BF16),
        vmem((seq, width), F32),
        vmem((seq, width), BF16),
        vmem((width, seq), BF16),
        vmem((inner, seq), BF16),
        vmem((width // side, n_dp * seq), BF16),
        vmem((inner, n_dp * seq), BF16),
        vmem((n_dp * seq, 3 * inner // side), BF16),
        vmem((n_dp * seq, width // n_dp), BF16),
        vmem((side, seq, 3 * inner // side), BF16),
        vmem((inner, width // n_dp), BF16),
        dma((w_blk,)),
        dma,
        dma((3 + 2 * CHUNKS,)),
        dma((5,)),
        dma((CHUNKS,)),
        dma((CHUNKS,)),
        dma((CHUNKS,)),
        dma((CHUNKS,)),
        dma((n_dp,)),
        dma((n_dp,)),
        dma((n_dp,)),
        dma((n_dp,)),
        dma((CHUNKS, n_dp)),
        dma((CHUNKS, n_dp)),
        dma((n_dp,)),
        dma((n_dp,)),
        dma((side,)),
        dma((side,)),
    ]
    return pl.pallas_call(
        kernel,
        out_shape=(
            jax.ShapeDtypeStruct((1, seq, width), BF16),
            jax.ShapeDtypeStruct((1, seq, width), BF16),
            jax.ShapeDtypeStruct((1, width // n_dp, 3 * inner), BF16),
            jax.ShapeDtypeStruct((1, inner, width // n_dp), BF16),
        ),
        in_specs=[pl.BlockSpec(memory_space=pltpu.SMEM)] + [any_space] * 4,
        out_specs=[any_space] * 4,
        scratch_shapes=scratch,
        compiler_params=pltpu.CompilerParams(
            collective_id=0, has_side_effects=True, vmem_limit_bytes=60 << 20
        ),
    )(slice_lengths, tokens_in, cotangent, in_weights, out_weights)


def solution(mesh):
    placed = (
        P("dp", None),
        P("dp", None),
        P("section", None, None),
        P("section", None, None),
        P("dp", None),
    )
    return jax.shard_map(
        on_device,
        mesh=mesh,
        in_specs=placed,
        out_specs=(
            P("section", "dp", None),
            P("section", "dp", None),
            P("section", "dp", None),
            P("section", None, "dp"),
        ),
        check_vma=False,
    )
```

time: 1350 us -> 231 us (0.17)
  the two profiles are of different devices: /device:TPU:0 before, /device:TPU:27 now
where the time goes in v1:
time: 231 us; the launch traced here: 230 us
  Pallas kernels  222 us (96%)
  local copies, waits for them, and re-layouts  7.49 us (3%)
    pallas_call x1, Pallas kernels, on_device(): pl.pallas_call(kernel, out_shape=(jax.ShapeDtypeStruct((1, seq, width), B...  222 us
    unnamed x4, local copies, waits for them, and re-layouts  7.49 us

profile of v1, /device:TPU:27, one launch (start us, length us, event | category | flops | bytes accessed | tf_op | source)
XLA Modules:
  0.0 230.2 jit_solution(130219396675577291)
XLA Ops:
  0.6 222.1 %shard_map.84 = (bf16[1,128,2048]{2,1,0:T(8,128)(2,1)}, bf16[1,128,2048]{2,1,0:T(8,128)(2,1)}, bf16[1,128,3072]{2,1,0:T(8,128)(2,1)}, bf16[1,1024,128]{2,1,0:T(8,128)(2,1)}) custom-call(s32[1,8]{1,0:T(1,128)} %lens.1, bf16[128,2048]{1,0:T(8,128)(2,1)} %tok.1, bf16[128,2048]{1,0:T(8,128)(2,1)} %cot.1, bf16[1,2048,3072]{2,1,0:T(8,128)(2,1)} %win.1, ...), custom_call_target="tpu_custom_call" | custom-call | tf_op jit(solution)/shard_map/pallas_call | solution.py:562
  222.8 1.9 copy.13
  224.6 1.9 copy.14
  226.5 2.1 copy.15
  228.6 1.7 copy.16

commit v2 on v1

v2 whole, which is shorter than its diff:
```python
import math

import jax
import jax.numpy as jnp
from jax import lax
from jax.experimental import pallas as pl
from jax.experimental.pallas import tpu as pltpu
from jax.sharding import PartitionSpec as P

HS = 128
CHUNKS = 2
PIECES = 4
PARTS = 2
SUB = 16
MESH = pl.DeviceIdType.MESH
F32 = jnp.float32
BF16 = jnp.bfloat16


def padded(rows):
    missing = 128 - rows.shape[0]
    if missing <= 0:
        return rows
    return jnp.concatenate([rows, jnp.zeros((missing, rows.shape[1]), rows.dtype)], 0)


def product(rows, weight):
    return jnp.dot(padded(rows), weight, preferred_element_type=F32)[: rows.shape[0]]


def against_rows(left, right):
    return lax.dot_general(left, right, (((1,), (1,)), ((), ())), preferred_element_type=F32)


def over_rows(left, right):
    return lax.dot_general(left, right, (((0,), (0,)), ((), ())), preferred_element_type=F32)


def kernel(
    lens,
    tok,
    cot,
    win,
    wout,
    so,
    ig,
    gi,
    go,
    w_in,
    w_out,
    w_in_t,
    w_out_t,
    x_in,
    x_hat,
    inv_std,
    normed,
    proj,
    probs,
    mixed,
    out,
    up,
    grad_mixed,
    key_acc,
    val_acc,
    gp,
    gn,
    gin,
    n_t,
    m_t,
    up4,
    n_x,
    n_z,
    m_x,
    m_z,
    gp_x,
    gp_z,
    up_x,
    up_z,
    p_x,
    p_z,
    o_x,
    o_z,
    r_x,
    r_z,
    s_x,
    s_z,
    ro_x,
    ro_z,
    go_buf,
    win_sem,
    wout_sem,
    local_sem,
    own_sem,
    fwd_send,
    fwd_recv,
    bwd_send,
    bwd_recv,
    dp_send,
    dp_recv,
):
    sections = 8
    n_dp = 16
    side = 4
    sec = lax.axis_index("section")
    me = lax.axis_index("dp")
    my_z, my_x = me // side, lax.rem(me, side)
    seq, width = x_in.shape
    inner = w_out.shape[0]
    heads = inner // HS
    rows_c = seq // CHUNKS
    quarter = width // side
    half_cols = 3 * inner // 2
    gp_cols = half_cols // side
    half_in = inner // 2
    w_blk = win_sem.shape[0]
    w_cols = 3 * inner // w_blk
    scale = 1.0 / math.sqrt(HS)
    grad_scale = 1.0 / math.sqrt(seq * n_dp)
    piece_cols = width // PIECES

    def aligned(index, size):
        return pl.ds(pl.multiple_of(index * size, size), size)

    def win_copy(j):
        cols = pl.ds(j * w_cols, w_cols)
        return pltpu.make_async_copy(win.at[0, :, cols], w_in.at[:, cols], win_sem.at[j])

    wout_copy = pltpu.make_async_copy(wout.at[0], w_out, wout_sem)
    tok_copy = pltpu.make_async_copy(tok, x_in, local_sem.at[0])
    cot_copy = pltpu.make_async_copy(cot, up, local_sem.at[1])

    @pl.when(sec == 0)
    def _():
        tok_copy.start()

    @pl.when(sec == sections - 1)
    def _():
        cot_copy.start()

    for j in range(w_blk):
        win_copy(j).start()
    wout_copy.start()

    def at_x(d):
        return my_z * side + lax.rem(my_x + d, side)

    def at_z(d):
        return lax.rem(my_z + d, side) * side + my_x

    barrier = pltpu.get_barrier_semaphore()
    for d in (1, 2, 3):
        for to in (at_x(d), at_z(d)):
            pl.semaphore_signal(barrier, inc=1, device_id={"dp": to}, device_id_type=MESH)
    for step in (1, sections - 1):
        pl.semaphore_signal(
            barrier,
            inc=1,
            device_id={"section": lax.rem(sec + step, sections)},
            device_id_type=MESH,
        )

    row_at = lax.broadcasted_iota(jnp.int32, (seq, seq), 0)
    col_at = lax.broadcasted_iota(jnp.int32, (seq, seq), 1)
    causal = col_at <= row_at
    if CHUNKS > 1:
        proj[...] = jnp.zeros_like(proj)
    pl.semaphore_wait(barrier, 8)

    def transpose_weights():
        blk = 512

        def turn(source, dest):
            rows, cols = source.shape
            wide = cols // blk

            def one(i, _):
                r = pl.multiple_of((i // wide) * blk, blk)
                c = pl.multiple_of(lax.rem(i, wide) * blk, blk)
                dest[pl.ds(c, blk), pl.ds(r, blk)] = source[pl.ds(r, blk), pl.ds(c, blk)].T
                return 0

            lax.fori_loop(0, (rows // blk) * wide, one, 0)

        turn(w_in, w_in_t)
        turn(w_out, w_out_t)

    @pl.when(sec > 0)
    def _():
        for j in range(w_blk):
            win_copy(j).wait()
        wout_copy.wait()

    @pl.when(sec >= sections // 2)
    def _():
        transpose_weights()

    def fwd_hop(c, j):
        at = (pl.ds(c * rows_c, rows_c), pl.ds(j * piece_cols, piece_cols))
        return pltpu.make_async_remote_copy(
            src_ref=out.at[at],
            dst_ref=x_in.at[at],
            send_sem=fwd_send.at[c, j],
            recv_sem=fwd_recv.at[c, j],
            device_id={"section": lax.rem(sec + 1, sections)},
            device_id_type=MESH,
        )

    def so_copy(c):
        rows = pl.ds(c * rows_c, rows_c)
        return pltpu.make_async_copy(out.at[rows], so.at[0, rows], local_sem.at[2 + c])

    @pl.when(sec == 0)
    def _():
        tok_copy.wait()

    every = range(heads)
    q_at = [slice(h * HS, (h + 1) * HS) for h in every]
    k_at = [slice(inner + h * HS, inner + (h + 1) * HS) for h in every]
    v_at = [slice(2 * inner + h * HS, 2 * inner + (h + 1) * HS) for h in every]

    for c in range(CHUNKS):
        r0 = c * rows_c
        rows = slice(r0, r0 + rows_c)

        @pl.when(sec > 0)
        def _():
            for j in range(PIECES):
                fwd_hop(c, j).wait_recv()

        for r in range(r0, r0 + rows_c, SUB):
            sub = slice(r, r + SUB)
            values = x_in[sub, :].astype(F32)
            centre = jnp.mean(values, -1, keepdims=True)
            shifted = values - centre
            inv = lax.rsqrt(jnp.mean(shifted * shifted, -1, keepdims=True) + 1e-05)
            hat = shifted * inv
            x_hat[sub, :] = hat
            inv_std[sub, :] = jnp.broadcast_to(inv, (SUB, 128))
            normed[sub, :] = hat.astype(BF16)

        for j in range(w_blk):
            if c == 0:

                @pl.when(sec == 0)
                def _():
                    win_copy(j).wait()

            cols = slice(j * w_cols, (j + 1) * w_cols)
            proj[rows, cols] = product(normed[rows, :], w_in[:, cols]).astype(BF16)

        seen = causal[rows, :]
        scores = [against_rows(proj[rows, q_at[h]], proj[:, k_at[h]]) for h in every]
        scores = [jnp.where(seen, a, -jnp.inf) for a in scores]
        top = [jnp.max(a, -1, keepdims=True) for a in scores]
        weight = [jnp.exp((a - t) * scale) for a, t in zip(scores, top)]
        total = [1.0 / jnp.sum(a, -1, keepdims=True) for a in weight]
        p = [a * t for a, t in zip(weight, total)]
        for h in every:
            probs[h, rows, :] = p[h]
        mixes = [
            jnp.dot(p[h].astype(BF16), proj[:, v_at[h]], preferred_element_type=F32) for h in every
        ]
        for h in every:
            mixed[rows, q_at[h]] = mixes[h].astype(BF16)

        if c == 0:

            @pl.when(sec == 0)
            def _():
                wout_copy.wait()

        for j in range(PIECES):
            cols = slice(j * piece_cols, (j + 1) * piece_cols)
            out[rows, cols] = (
                x_in[rows, cols].astype(F32) + product(mixed[rows, :], w_out[:, cols])
            ).astype(BF16)

            @pl.when(sec < sections - 1)
            def _():
                fwd_hop(c, j).start()

        so_copy(c).start()

    n_kind, m_kind, up_kind, r_kind, ro_kind, fin_kind, gp_kind = range(7)
    mine_x, mine_z = aligned(my_x, seq), aligned(my_z, seq)

    def dp_copy(src, dst, kind, axis, d):
        return pltpu.make_async_remote_copy(
            src_ref=src,
            dst_ref=dst,
            send_sem=dp_send.at[kind, axis, d],
            recv_sem=dp_recv.at[kind, axis, d],
            device_id={"dp": at_z(d) if axis else at_x(d)},
            device_id_type=MESH,
        )

    def n_copies(d):
        return (
            dp_copy(n_t, n_x.at[:, mine_x], n_kind, 0, d),
            dp_copy(n_t, n_z.at[:, mine_z], n_kind, 1, d),
        )

    def m_copies(d):
        return (
            dp_copy(m_t.at[:half_in], m_x.at[:, mine_x], m_kind, 0, d),
            dp_copy(m_t.at[half_in:], m_z.at[:, mine_z], m_kind, 1, d),
        )

    def up_copies(d):
        x, z = lax.rem(my_x + d, side), lax.rem(my_z + d, side)
        return (
            dp_copy(up4.at[:, x], up_x.at[:, mine_x], up_kind, 0, d),
            dp_copy(up4.at[z], up_z.at[:, mine_z], up_kind, 1, d),
        )

    def gp_copies(c, d):
        x, z = lax.rem(my_x + d, side), lax.rem(my_z + d, side)
        rows = pl.ds(c * rows_c, rows_c)
        z_cols = pl.ds(pl.multiple_of(half_cols + z * gp_cols, gp_cols), gp_cols)
        return (
            dp_copy(
                gp.at[rows, aligned(x, gp_cols)],
                gp_x.at[my_x, rows],
                gp_kind + c,
                0,
                d,
            ),
            dp_copy(gp.at[rows, z_cols], gp_z.at[my_z, rows], gp_kind + c, 1, d),
        )

    def r_copies(d):
        x, z = lax.rem(my_x + d, side), lax.rem(my_z + d, side)
        return (
            dp_copy(p_z.at[x], r_z.at[d], r_kind, 0, d),
            dp_copy(p_x.at[z], r_x.at[d], r_kind, 1, d),
        )

    def ro_copies(d):
        x, z = lax.rem(my_x + d, side), lax.rem(my_z + d, side)
        return (
            dp_copy(o_z.at[x], ro_z.at[d], ro_kind, 0, d),
            dp_copy(o_x.at[z], ro_x.at[d], ro_kind, 1, d),
        )

    fin_x = gi.at[0, :, aligned(my_x, gp_cols)]
    fin_z = gi.at[0, :, pl.ds(pl.multiple_of(half_cols + my_z * gp_cols, gp_cols), gp_cols)]

    def fin_copies(d):
        x, z = lax.rem(my_x + d, side), lax.rem(my_z + d, side)
        return (
            dp_copy(s_x.at[x], fin_x, fin_kind, 0, d),
            dp_copy(s_z.at[z], fin_z, fin_kind, 1, d),
        )

    def start(*pairs):
        for pair in pairs:
            for copy in pair:
                copy.start()

    def arrived(copies):
        for d in (1, 3, 2):
            for copy in copies(d):
                copy.wait_recv()

    def send_forward_operands():
        for r in range(0, width, 512):
            n_t[r : r + 512, :] = normed[:, r : r + 512].T
        for r in range(0, inner, 512):
            m_t[r : r + 512, :] = mixed[:, r : r + 512].T
        for d in (2, 1, 3):
            start(n_copies(d), m_copies(d))

    @pl.when(sec < sections - 1)
    def _():
        send_forward_operands()

    @pl.when(sec < sections // 2)
    def _():
        transpose_weights()

    row_slice = jnp.zeros((seq, seq), jnp.int32)
    col_slice = jnp.zeros((seq, seq), jnp.int32)
    end = jnp.int32(0)
    for j in range(lens.shape[1]):
        end = end + lens[0, j]
        row_slice = row_slice + jnp.where(row_at >= end, 1, 0)
        col_slice = col_slice + jnp.where(col_at >= end, 1, 0)
    same = row_slice == col_slice

    def bwd_hop(c):
        rows = pl.ds(c * rows_c, rows_c)
        return pltpu.make_async_remote_copy(
            src_ref=gin.at[rows],
            dst_ref=up.at[rows],
            send_sem=bwd_send.at[c],
            recv_sem=bwd_recv.at[c],
            device_id={"section": lax.rem(sec + sections - 1, sections)},
            device_id_type=MESH,
        )

    def ig_copy(c):
        rows = pl.ds(c * rows_c, rows_c)
        return pltpu.make_async_copy(gin.at[rows], ig.at[0, rows], local_sem.at[2 + CHUNKS + c])

    @pl.when(sec == sections - 1)
    def _():
        cot_copy.wait()

    for c in reversed(range(CHUNKS)):
        r0 = c * rows_c
        rows = slice(r0, r0 + rows_c)

        @pl.when(sec < sections - 1)
        def _():
            bwd_hop(c).wait_recv()

        for j in range(0, inner, 512):
            cols = slice(j, j + 512)
            grad_mixed[rows, cols] = product(up[rows, :], w_out_t[:, cols]).astype(BF16)

        live = same[rows, :]
        grad_p = [against_rows(grad_mixed[rows, q_at[h]], proj[:, v_at[h]]) for h in every]
        p = [probs[h, rows, :] for h in every]
        own_p = [jnp.where(live, a, 0.0).astype(BF16) for a in p]
        grad_v = [over_rows(own_p[h], grad_mixed[rows, q_at[h]]) for h in every]
        weighted = [a * b for a, b in zip(p, grad_p)]
        delta = [jnp.sum(a, -1, keepdims=True) for a in weighted]
        grad_s = [a * (b - t) for a, b, t in zip(p, grad_p, delta)]
        grad_q = [
            jnp.dot(grad_s[h].astype(BF16), proj[:, k_at[h]], preferred_element_type=F32)
            for h in every
        ]
        own_s = [jnp.where(live, a, 0.0).astype(BF16) for a in grad_s]
        grad_k = [over_rows(own_s[h], proj[rows, q_at[h]]) for h in every]
        for h in every:
            gk, gv = grad_k[h], grad_v[h]
            if c < CHUNKS - 1:
                gk = gk[: r0 + rows_c] + key_acc[: r0 + rows_c, q_at[h]]
                gv = gv[: r0 + rows_c] + val_acc[: r0 + rows_c, q_at[h]]
            if c > 0:
                key_acc[:r0, q_at[h]] = gk[:r0]
                val_acc[:r0, q_at[h]] = gv[:r0]
            gp[rows, q_at[h]] = (grad_q[h] * scale).astype(BF16)
            gp[rows, k_at[h]] = (gk[rows] * scale).astype(BF16)
            gp[rows, v_at[h]] = gv[rows].astype(BF16)

        @pl.when(sec == 0)
        def _():
            for d in (2, 1, 3):
                start(gp_copies(c, d))

        for j in range(0, width, 512):
            cols = slice(j, j + 512)
            gn[rows, cols] = product(gp[rows, :], w_in_t[:, cols])

        for r in range(r0, r0 + rows_c, SUB):
            sub = slice(r, r + SUB)
            g = gn[sub, :]
            hat = x_hat[sub, :]
            mean_g = jnp.mean(g, -1, keepdims=True)
            mean_gh = jnp.mean(g * hat, -1, keepdims=True)
            grad = inv_std[sub, :1] * (g - mean_g - hat * mean_gh)
            gin[sub, :] = (up[sub, :].astype(F32) + grad).astype(BF16)

        @pl.when(sec > 0)
        def _():
            bwd_hop(c).start()
            for d in (2, 1, 3):
                start(gp_copies(c, d))

        ig_copy(c).start()

    for b in range(n_dp):
        up4[b // side, b % side] = up[:, b * seq : (b + 1) * seq]
    for d in (2, 1, 3):
        start(up_copies(d))

    @pl.when(sec == sections - 1)
    def _():
        send_forward_operands()

    n_x[:, mine_x] = n_t[...]
    n_z[:, mine_z] = n_t[...]
    m_x[:, mine_x] = m_t[:half_in]
    m_z[:, mine_z] = m_t[half_in:]
    gp_x[my_x] = gp[:, aligned(my_x, gp_cols)]
    gp_z[my_z] = gp[:, pl.ds(pl.multiple_of(half_cols + my_z * gp_cols, gp_cols), gp_cols)]
    for b in range(side):
        up_x[b, mine_x] = up4[b, my_x]
        up_z[b, mine_z] = up4[my_z, b]

    arrived(n_copies)
    for c in reversed(range(CHUNKS)):
        arrived(lambda d: gp_copies(c, d))
    group = side * seq
    gx = gp_x[...].reshape(group, gp_cols)
    gz = gp_z[...].reshape(group, gp_cols)
    for d in (2, 1, 3, 0):
        x, z = lax.rem(my_x + d, side), lax.rem(my_z + d, side)
        first = jnp.dot(n_x[aligned(z, quarter), :], gx, preferred_element_type=F32) * grad_scale
        p_x[z] = first.astype(BF16)
        if d:
            r_copies(d)[1].start()
        for b in range(side):
            at = pl.ds(pl.multiple_of(b * quarter + x * seq, seq), seq)
            second = jnp.dot(n_z[at, :], gz, preferred_element_type=F32) * grad_scale
            p_z[x, b] = second.astype(BF16)
        if d:
            r_copies(d)[0].start()

    arrived(m_copies)
    arrived(up_copies)
    for d in (2, 1, 3, 0):
        x, z = lax.rem(my_x + d, side), lax.rem(my_z + d, side)
        first = jnp.dot(m_x[...], up_x[z], preferred_element_type=F32) * grad_scale
        second = jnp.dot(m_z[...], up_z[x], preferred_element_type=F32) * grad_scale
        o_x[z] = first.astype(BF16)
        o_z[x] = second.astype(BF16)
        if d:
            start(ro_copies(d))

    arrived(r_copies)
    for b in range(side):
        at = slice(b * seq, (b + 1) * seq)
        first = p_x[my_z, at].astype(F32)
        second = p_z[my_x, b].astype(F32)
        for d in (1, 2, 3):
            first = first + r_x[d, at].astype(F32)
            second = second + r_z[d, b].astype(F32)
        s_x[b] = first.astype(BF16)
        s_z[b] = second.astype(BF16)
    for d in (2, 1, 3):
        start(fin_copies(d))
    own_x = pltpu.make_async_copy(s_x.at[my_x], fin_x, own_sem.at[0])
    own_z = pltpu.make_async_copy(s_z.at[my_z], fin_z, own_sem.at[1])
    own_x.start()
    own_z.start()

    arrived(ro_copies)
    first = o_x[my_z].astype(F32)
    second = o_z[my_x].astype(F32)
    for d in (1, 2, 3):
        first = first + ro_x[d].astype(F32)
        second = second + ro_z[d].astype(F32)
    go_buf[:half_in] = first.astype(BF16)
    go_buf[half_in:] = second.astype(BF16)
    go_copy = pltpu.make_async_copy(go_buf, go.at[0], local_sem.at[2 + 2 * CHUNKS])
    go_copy.start()

    for d in (1, 2, 3):
        pairs = [n_copies(d), m_copies(d), up_copies(d), r_copies(d), ro_copies(d)]
        pairs += [gp_copies(c, d) for c in range(CHUNKS)]
        for pair in pairs:
            for copy in pair:
                copy.wait_send()
    for c in range(CHUNKS):

        @pl.when(sec < sections - 1)
        def _():
            for j in range(PIECES):
                fwd_hop(c, j).wait_send()

        @pl.when(sec > 0)
        def _():
            bwd_hop(c).wait_send()

        so_copy(c).wait()
        ig_copy(c).wait()
    go_copy.wait()
    own_x.wait()
    own_z.wait()
    for d in (1, 2, 3):
        for copy in fin_copies(d):
            copy.wait()


def hand_on(*refs):
    count = (len(refs) - 2) // 3
    sems_in, sems_out = refs[-2:]
    loads, stores = [], []
    for i in range(count):
        source, dest, held = refs[i], refs[count + i], refs[2 * count + i]
        rows = source.shape[1] // PARTS
        for j in range(PARTS):
            at, slot = pl.ds(j * rows, rows), i * PARTS + j
            loads.append(pltpu.make_async_copy(source.at[0, at], held.at[at], sems_in.at[slot]))
            stores.append(pltpu.make_async_copy(held.at[at], dest.at[0, at], sems_out.at[slot]))
    for copy in loads:
        copy.start()
    for load, store in zip(loads, stores):
        load.wait()
        store.start()
    for copy in stores:
        copy.wait()


def on_device(tokens_in, cotangent, in_weights, out_weights, slice_lengths):
    seq, width = tokens_in.shape
    inner = out_weights.shape[1]
    heads = inner // HS
    n_dp, side = 16, 4
    group = side * seq
    gp_cols = 3 * inner // 8
    any_space = pl.BlockSpec(memory_space=pl.ANY)
    vmem = pltpu.VMEM
    dma = pltpu.SemaphoreType.DMA
    w_blk = 4
    scratch = [
        vmem((width, 3 * inner), BF16),
        vmem((inner, width), BF16),
        vmem((3 * inner, width), BF16),
        vmem((width, inner), BF16),
        vmem((seq, width), BF16),
        vmem((seq, width), F32),
        vmem((seq, 128), F32),
        vmem((seq, width), BF16),
        vmem((seq, 3 * inner), BF16),
        vmem((heads, seq, seq), F32),
        vmem((seq, inner), BF16),
        vmem((seq, width), BF16),
        vmem((seq, width), BF16),
        vmem((seq, inner), BF16),
        vmem((seq, inner), F32),
        vmem((seq, inner), F32),
        vmem((seq, 3 * inner), BF16),
        vmem((seq, width), F32),
        vmem((seq, width), BF16),
        vmem((width, seq), BF16),
        vmem((inner, seq), BF16),
        vmem((side, side, seq, width // n_dp), BF16),
        vmem((width, group), BF16),
        vmem((width, group), BF16),
        vmem((inner // 2, group), BF16),
        vmem((inner // 2, group), BF16),
        vmem((side, seq, gp_cols), BF16),
        vmem((side, seq, gp_cols), BF16),
        vmem((side, group, width // n_dp), BF16),
        vmem((side, group, width // n_dp), BF16),
        vmem((side, width // side, gp_cols), BF16),
        vmem((side, side, seq, gp_cols), BF16),
        vmem((side, inner // 2, width // n_dp), BF16),
        vmem((side, inner // 2, width // n_dp), BF16),
        vmem((side, width // side, gp_cols), BF16),
        vmem((side, side, seq, gp_cols), BF16),
        vmem((side, seq, gp_cols), BF16),
        vmem((side, seq, gp_cols), BF16),
        vmem((side, inner // 2, width // n_dp), BF16),
        vmem((side, inner // 2, width // n_dp), BF16),
        vmem((inner, width // n_dp), BF16),
        dma((w_blk,)),
        dma,
        dma((3 + 2 * CHUNKS,)),
        dma((2,)),
        dma((CHUNKS, PIECES)),
        dma((CHUNKS, PIECES)),
        dma((CHUNKS,)),
        dma((CHUNKS,)),
        dma((6 + CHUNKS, 2, side)),
        dma((6 + CHUNKS, 2, side)),
    ]
    shapes = (
        jax.ShapeDtypeStruct((1, seq, width), BF16),
        jax.ShapeDtypeStruct((1, seq, width), BF16),
        jax.ShapeDtypeStruct((1, width // n_dp, 3 * inner), BF16),
        jax.ShapeDtypeStruct((1, inner, width // n_dp), BF16),
    )
    results = pl.pallas_call(
        kernel,
        out_shape=shapes,
        in_specs=[pl.BlockSpec(memory_space=pltpu.SMEM)] + [any_space] * 4,
        out_specs=[any_space] * 4,
        scratch_shapes=scratch,
        compiler_params=pltpu.CompilerParams(
            collective_id=0, has_side_effects=True, vmem_limit_bytes=62 << 20
        ),
    )(slice_lengths, tokens_in, cotangent, in_weights, out_weights)
    return pl.pallas_call(
        hand_on,
        out_shape=shapes,
        in_specs=[any_space] * 4,
        out_specs=[any_space] * 4,
        scratch_shapes=[vmem(s.shape[1:], BF16) for s in shapes]
        + [dma((4 * PARTS,)), dma((4 * PARTS,))],
    )(*results)


def solution(mesh):
    placed = (
        P("dp", None),
        P("dp", None),
        P("section", None, None),
        P("section", None, None),
        P("dp", None),
    )
    return jax.shard_map(
        on_device,
        mesh=mesh,
        in_specs=placed,
        out_specs=(
            P("section", "dp", None),
            P("section", "dp", None),
            P("section", "dp", None),
            P("section", None, "dp"),
        ),
        check_vma=False,
    )
```

time: 231 us -> 152 us (0.66)
  the two profiles are of different devices: /device:TPU:27 before, /device:TPU:0 now
where the time goes in v2:
time: 152 us
  Pallas kernels  151 us (99%)
    pallas_call x1, Pallas kernels, on_device(): pl.pallas_call(kernel, out_shape=shapes, in_specs=[pl.BlockSpec(memory_sp...  149 us

profile of v2, /device:TPU:0, one launch (start us, length us, event | category | flops | bytes accessed | tf_op | source)
XLA Modules:
  0.0 151.8 jit_solution(10859495748816133487)
XLA Ops:
  0.6 148.5 %shard_map.84 = (bf16[1,128,2048]{2,1,0:T(8,128)(2,1)}, bf16[1,128,2048]{2,1,0:T(8,128)(2,1)}, bf16[1,128,3072]{2,1,0:T(8,128)(2,1)}, bf16[1,1024,128]{2,1,0:T(8,128)(2,1)}) custom-call(s32[1,8]{1,0:T(1,128)} %lens.1, bf16[128,2048]{1,0:T(8,128)(2,1)} %tok.1, bf16[128,2048]{1,0:T(8,128)(2,1)} %cot.1, bf16[1,2048,3072]{2,1,0:T(8,128)(2,1)} %win.1, ...), custom_call_target="tpu_custom_call" | custom-call | tf_op jit(solution)/shard_map/pallas_call | solution.py:667
  149.2 2.4 %shard_map.85 = (bf16[1,128,2048]{2,1,0:T(8,128)(2,1)}, bf16[1,128,2048]{2,1,0:T(8,128)(2,1)}, bf16[1,128,3072]{2,1,0:T(8,128)(2,1)}, bf16[1,1024,128]{2,1,0:T(8,128)(2,1)}) custom-call(bf16[1,128,2048]{2,1,0:T(8,128)(2,1)} %get-tuple-element.8.refs_0_, bf16[1,128,2048]{2,1,0:T(8,128)(2,1)} %get-tuple-element.9.refs_1_, ...), custom_call_target="tpu_custom_call" | custom-call | tf_op jit(solution)/shard_map/pallas_call | solution.py:677

commit v3 on v2

--- a/solution.py
+++ b/solution.py
@@ -9,7 +9,7 @@
 
 HS = 128
 CHUNKS = 2
-PIECES = 4
+PIECES = 2
 PARTS = 2
 SUB = 16
 MESH = pl.DeviceIdType.MESH
@@ -37,7 +37,7 @@
 
 
 def kernel(
-    lens,
+    lens_in,
     tok,
     cot,
     win,
@@ -87,8 +87,10 @@
     ro_x,
     ro_z,
     go_buf,
+    lens,
     win_sem,
     wout_sem,
+    tok_sem,
     local_sem,
     own_sem,
     fwd_send,
@@ -104,7 +106,7 @@
     sec = lax.axis_index("section")
     me = lax.axis_index("dp")
     my_z, my_x = me // side, lax.rem(me, side)
-    seq, width = x_in.shape
+    _, seq, width = x_in.shape
     inner = w_out.shape[0]
     heads = inner // HS
     rows_c = seq // CHUNKS
@@ -113,7 +115,6 @@
     gp_cols = half_cols // side
     half_in = inner // 2
     w_blk = win_sem.shape[0]
-    w_cols = 3 * inner // w_blk
     scale = 1.0 / math.sqrt(HS)
     grad_scale = 1.0 / math.sqrt(seq * n_dp)
     piece_cols = width // PIECES
@@ -121,17 +122,29 @@
     def aligned(index, size):
         return pl.ds(pl.multiple_of(index * size, size), size)
 
+    w_starts = [part * inner + g * half_in for g in (0, 1) for part in range(3)]
+
     def win_copy(j):
-        cols = pl.ds(j * w_cols, w_cols)
+        cols = pl.ds(w_starts[j], half_in)
         return pltpu.make_async_copy(win.at[0, :, cols], w_in.at[:, cols], win_sem.at[j])
 
-    wout_copy = pltpu.make_async_copy(wout.at[0], w_out, wout_sem)
-    tok_copy = pltpu.make_async_copy(tok, x_in, local_sem.at[0])
-    cot_copy = pltpu.make_async_copy(cot, up, local_sem.at[1])
+    def wout_copy(j):
+        cols = pl.ds(j * (width // 2), width // 2)
+        return pltpu.make_async_copy(wout.at[0, :, cols], w_out.at[:, cols], wout_sem.at[j])
+
+    def tok_copy(c):
+        rows = pl.ds(c * rows_c, rows_c)
+        return pltpu.make_async_copy(tok.at[rows], x_in.at[0, rows], tok_sem.at[c])
+
+    lens_copy = pltpu.make_async_copy(lens_in, lens, local_sem.at[0])
+    cot_copy = pltpu.make_async_copy(cot, up.at[0], local_sem.at[1])
+    in_slot = jnp.where(sec == 0, 0, 1)
+    up_slot = jnp.where(sec == sections - 1, 0, 1)
 
     @pl.when(sec == 0)
     def _():
-        tok_copy.start()
+        for c in range(CHUNKS):
+            tok_copy(c).start()
 
     @pl.when(sec == sections - 1)
     def _():
@@ -139,7 +152,9 @@
 
     for j in range(w_blk):
         win_copy(j).start()
-    wout_copy.start()
+    for j in (0, 1):
+        wout_copy(j).start()
+    lens_copy.start()
 
     def at_x(d):
         return my_z * side + lax.rem(my_x + d, side)
@@ -164,7 +179,6 @@
     causal = col_at <= row_at
     if CHUNKS > 1:
         proj[...] = jnp.zeros_like(proj)
-    pl.semaphore_wait(barrier, 8)
 
     def transpose_weights():
         blk = 512
@@ -188,7 +202,8 @@
     def _():
         for j in range(w_blk):
             win_copy(j).wait()
-        wout_copy.wait()
+        for j in (0, 1):
+            wout_copy(j).wait()
 
     @pl.when(sec >= sections // 2)
     def _():
@@ -198,7 +213,7 @@
         at = (pl.ds(c * rows_c, rows_c), pl.ds(j * piece_cols, piece_cols))
         return pltpu.make_async_remote_copy(
             src_ref=out.at[at],
-            dst_ref=x_in.at[at],
+            dst_ref=x_in.at[1].at[at],
             send_sem=fwd_send.at[c, j],
             recv_sem=fwd_recv.at[c, j],
             device_id={"section": lax.rem(sec + 1, sections)},
@@ -209,11 +224,7 @@
         rows = pl.ds(c * rows_c, rows_c)
         return pltpu.make_async_copy(out.at[rows], so.at[0, rows], local_sem.at[2 + c])
 
-    @pl.when(sec == 0)
-    def _():
-        tok_copy.wait()
-
-    every = range(heads)
+    every = list(range(heads))
     q_at = [slice(h * HS, (h + 1) * HS) for h in every]
     k_at = [slice(inner + h * HS, inner + (h + 1) * HS) for h in every]
     v_at = [slice(2 * inner + h * HS, 2 * inner + (h + 1) * HS) for h in every]
@@ -227,9 +238,13 @@
             for j in range(PIECES):
                 fwd_hop(c, j).wait_recv()
 
+        @pl.when(sec == 0)
+        def _():
+            tok_copy(c).wait()
+
         for r in range(r0, r0 + rows_c, SUB):
             sub = slice(r, r + SUB)
-            values = x_in[sub, :].astype(F32)
+            values = x_in[in_slot, sub, :].astype(F32)
             centre = jnp.mean(values, -1, keepdims=True)
             shifted = values - centre
             inv = lax.rsqrt(jnp.mean(shifted * shifted, -1, keepdims=True) + 1e-05)
@@ -238,50 +253,61 @@
             inv_std[sub, :] = jnp.broadcast_to(inv, (SUB, 128))
             normed[sub, :] = hat.astype(BF16)
 
-        for j in range(w_blk):
-            if c == 0:
-
-                @pl.when(sec == 0)
-                def _():
+        def project(blocks, loading):
+            for j in blocks:
+                if loading:
                     win_copy(j).wait()
-
-            cols = slice(j * w_cols, (j + 1) * w_cols)
-            proj[rows, cols] = product(normed[rows, :], w_in[:, cols]).astype(BF16)
-
-        seen = causal[rows, :]
-        scores = [against_rows(proj[rows, q_at[h]], proj[:, k_at[h]]) for h in every]
-        scores = [jnp.where(seen, a, -jnp.inf) for a in scores]
-        top = [jnp.max(a, -1, keepdims=True) for a in scores]
-        weight = [jnp.exp((a - t) * scale) for a, t in zip(scores, top)]
-        total = [1.0 / jnp.sum(a, -1, keepdims=True) for a in weight]
-        p = [a * t for a, t in zip(weight, total)]
-        for h in every:
-            probs[h, rows, :] = p[h]
-        mixes = [
-            jnp.dot(p[h].astype(BF16), proj[:, v_at[h]], preferred_element_type=F32) for h in every
-        ]
-        for h in every:
-            mixed[rows, q_at[h]] = mixes[h].astype(BF16)
+                cols = slice(w_starts[j], w_starts[j] + half_in)
+                proj[rows, cols] = product(normed[rows, :], w_in[:, cols]).astype(BF16)
+
+        def attend(group):
+            seen = causal[rows, :]
+            scores = [against_rows(proj[rows, q_at[h]], proj[:, k_at[h]]) for h in group]
+            scores = [jnp.where(seen, a, -jnp.inf) for a in scores]
+            top = [jnp.max(a, -1, keepdims=True) for a in scores]
+            weight = [jnp.exp((a - t) * scale) for a, t in zip(scores, top)]
+            total = [1.0 / jnp.sum(a, -1, keepdims=True) for a in weight]
+            p = [a * t for a, t in zip(weight, total)]
+            for h, a in zip(group, p):
+                probs[h, rows, :] = a
+            mixes = [
+                jnp.dot(a.astype(BF16), proj[:, v_at[h]], preferred_element_type=F32)
+                for h, a in zip(group, p)
+            ]
+            for h, a in zip(group, mixes):
+                mixed[rows, q_at[h]] = a.astype(BF16)
 
         if c == 0:
 
             @pl.when(sec == 0)
             def _():
-                wout_copy.wait()
+                for g in (0, 1):
+                    project(range(3 * g, 3 * g + 3), True)
+                    attend(every[g * heads // 2 : (g + 1) * heads // 2])
+                for j in (0, 1):
+                    wout_copy(j).wait()
+
+            @pl.when(sec > 0)
+            def _():
+                project(range(w_blk), False)
+                attend(every)
+
+            pl.semaphore_wait(barrier, 8)
+        else:
+            project(range(w_blk), False)
+            attend(every)
 
         for j in range(PIECES):
             cols = slice(j * piece_cols, (j + 1) * piece_cols)
             out[rows, cols] = (
-                x_in[rows, cols].astype(F32) + product(mixed[rows, :], w_out[:, cols])
+                x_in[in_slot, rows, cols].astype(F32) + product(mixed[rows, :], w_out[:, cols])
             ).astype(BF16)
-
-            @pl.when(sec < sections - 1)
-            def _():
-                fwd_hop(c, j).start()
+            fwd_hop(c, j).start()
 
         so_copy(c).start()
 
-    n_kind, m_kind, up_kind, r_kind, ro_kind, fin_kind, gp_kind = range(7)
+    n_kind, m_kind, r_kind, ro_kind, fin_kind, gp_kind = range(6)
+    up_kind = gp_kind + CHUNKS
     mine_x, mine_z = aligned(my_x, seq), aligned(my_z, seq)
 
     def dp_copy(src, dst, kind, axis, d):
@@ -306,11 +332,14 @@
             dp_copy(m_t.at[half_in:], m_z.at[:, mine_z], m_kind, 1, d),
         )
 
-    def up_copies(d):
+    def up_copies(c, d):
         x, z = lax.rem(my_x + d, side), lax.rem(my_z + d, side)
+        rows = pl.ds(c * rows_c, rows_c)
+        to_x = pl.ds(pl.multiple_of(my_x * seq + c * rows_c, rows_c), rows_c)
+        to_z = pl.ds(pl.multiple_of(my_z * seq + c * rows_c, rows_c), rows_c)
         return (
-            dp_copy(up4.at[:, x], up_x.at[:, mine_x], up_kind, 0, d),
-            dp_copy(up4.at[z], up_z.at[:, mine_z], up_kind, 1, d),
+            dp_copy(up4.at[:, x, rows], up_x.at[:, to_x], up_kind + c, 0, d),
+            dp_copy(up4.at[z, :, rows], up_z.at[:, to_z], up_kind + c, 1, d),
         )
 
     def gp_copies(c, d):
@@ -369,6 +398,10 @@
             m_t[r : r + 512, :] = mixed[:, r : r + 512].T
         for d in (2, 1, 3):
             start(n_copies(d), m_copies(d))
+        n_x[:, mine_x] = n_t[...]
+        n_z[:, mine_z] = n_t[...]
+        m_x[:, mine_x] = m_t[:half_in]
+        m_z[:, mine_z] = m_t[half_in:]
 
     @pl.when(sec < sections - 1)
     def _():
@@ -378,6 +411,7 @@
     def _():
         transpose_weights()
 
+    lens_copy.wait()
     row_slice = jnp.zeros((seq, seq), jnp.int32)
     col_slice = jnp.zeros((seq, seq), jnp.int32)
     end = jnp.int32(0)
@@ -391,7 +425,7 @@
         rows = pl.ds(c * rows_c, rows_c)
         return pltpu.make_async_remote_copy(
             src_ref=gin.at[rows],
-            dst_ref=up.at[rows],
+            dst_ref=up.at[1].at[rows],
             send_sem=bwd_send.at[c],
             recv_sem=bwd_recv.at[c],
             device_id={"section": lax.rem(sec + sections - 1, sections)},
@@ -416,7 +450,7 @@
 
         for j in range(0, inner, 512):
             cols = slice(j, j + 512)
-            grad_mixed[rows, cols] = product(up[rows, :], w_out_t[:, cols]).astype(BF16)
+            grad_mixed[rows, cols] = product(up[up_slot, rows, :], w_out_t[:, cols]).astype(BF16)
 
         live = same[rows, :]
         grad_p = [against_rows(grad_mixed[rows, q_at[h]], proj[:, v_at[h]]) for h in every]
@@ -444,10 +478,8 @@
             gp[rows, k_at[h]] = (gk[rows] * scale).astype(BF16)
             gp[rows, v_at[h]] = gv[rows].astype(BF16)
 
-        @pl.when(sec == 0)
-        def _():
-            for d in (2, 1, 3):
-                start(gp_copies(c, d))
+        for d in (2, 1, 3):
+            start(gp_copies(c, d))
 
         for j in range(0, width, 512):
             cols = slice(j, j + 512)
@@ -460,29 +492,19 @@
             mean_g = jnp.mean(g, -1, keepdims=True)
             mean_gh = jnp.mean(g * hat, -1, keepdims=True)
             grad = inv_std[sub, :1] * (g - mean_g - hat * mean_gh)
-            gin[sub, :] = (up[sub, :].astype(F32) + grad).astype(BF16)
-
-        @pl.when(sec > 0)
-        def _():
-            bwd_hop(c).start()
-            for d in (2, 1, 3):
-                start(gp_copies(c, d))
-
+            gin[sub, :] = (up[up_slot, sub, :].astype(F32) + grad).astype(BF16)
+
+        bwd_hop(c).start()
         ig_copy(c).start()
-
-    for b in range(n_dp):
-        up4[b // side, b % side] = up[:, b * seq : (b + 1) * seq]
-    for d in (2, 1, 3):
-        start(up_copies(d))
+        for b in range(n_dp):
+            up4[b // side, b % side, rows] = up[up_slot, rows, b * seq : (b + 1) * seq]
+        for d in (2, 1, 3):
+            start(up_copies(c, d))
 
     @pl.when(sec == sections - 1)
     def _():
         send_forward_operands()
 
-    n_x[:, mine_x] = n_t[...]
-    n_z[:, mine_z] = n_t[...]
-    m_x[:, mine_x] = m_t[:half_in]
-    m_z[:, mine_z] = m_t[half_in:]
     gp_x[my_x] = gp[:, aligned(my_x, gp_cols)]
     gp_z[my_z] = gp[:, pl.ds(pl.multiple_of(half_cols + my_z * gp_cols, gp_cols), gp_cols)]
     for b in range(side):
@@ -509,7 +531,8 @@
             r_copies(d)[0].start()
 
     arrived(m_copies)
-    arrived(up_copies)
+    for c in reversed(range(CHUNKS)):
+        arrived(lambda d: up_copies(c, d))
     for d in (2, 1, 3, 0):
         x, z = lax.rem(my_x + d, side), lax.rem(my_z + d, side)
         first = jnp.dot(m_x[...], up_x[z], preferred_element_type=F32) * grad_scale
@@ -519,18 +542,27 @@
         if d:
             start(ro_copies(d))
 
-    arrived(r_copies)
+    def landed(copies, axis):
+        for d in (1, 3, 2):
+            copies(d)[axis].wait_recv()
+
+    landed(r_copies, 1)
     for b in range(side):
         at = slice(b * seq, (b + 1) * seq)
-        first = p_x[my_z, at].astype(F32)
-        second = p_z[my_x, b].astype(F32)
+        total = p_x[my_z, at].astype(F32)
         for d in (1, 2, 3):
-            first = first + r_x[d, at].astype(F32)
-            second = second + r_z[d, b].astype(F32)
-        s_x[b] = first.astype(BF16)
-        s_z[b] = second.astype(BF16)
+            total = total + r_x[d, at].astype(F32)
+        s_x[b] = total.astype(BF16)
     for d in (2, 1, 3):
-        start(fin_copies(d))
+        fin_copies(d)[0].start()
+    landed(r_copies, 0)
+    for b in range(side):
+        total = p_z[my_x, b].astype(F32)
+        for d in (1, 2, 3):
+            total = total + r_z[d, b].astype(F32)
+        s_z[b] = total.astype(BF16)
+    for d in (2, 1, 3):
+        fin_copies(d)[1].start()
     own_x = pltpu.make_async_copy(s_x.at[my_x], fin_x, own_sem.at[0])
     own_z = pltpu.make_async_copy(s_z.at[my_z], fin_z, own_sem.at[1])
     own_x.start()
@@ -548,21 +580,26 @@
     go_copy.start()
 
     for d in (1, 2, 3):
-        pairs = [n_copies(d), m_copies(d), up_copies(d), r_copies(d), ro_copies(d)]
+        pairs = [n_copies(d), m_copies(d), r_copies(d), ro_copies(d)]
         pairs += [gp_copies(c, d) for c in range(CHUNKS)]
+        pairs += [up_copies(c, d) for c in range(CHUNKS)]
         for pair in pairs:
             for copy in pair:
                 copy.wait_send()
     for c in range(CHUNKS):
 
-        @pl.when(sec < sections - 1)
+        for j in range(PIECES):
+            fwd_hop(c, j).wait_send()
+        bwd_hop(c).wait_send()
+
+        @pl.when(sec == 0)
         def _():
             for j in range(PIECES):
-                fwd_hop(c, j).wait_send()
-
-        @pl.when(sec > 0)
+                fwd_hop(c, j).wait_recv()
+
+        @pl.when(sec == sections - 1)
         def _():
-            bwd_hop(c).wait_send()
+            bwd_hop(c).wait_recv()
 
         so_copy(c).wait()
         ig_copy(c).wait()
@@ -604,13 +641,12 @@
     any_space = pl.BlockSpec(memory_space=pl.ANY)
     vmem = pltpu.VMEM
     dma = pltpu.SemaphoreType.DMA
-    w_blk = 4
     scratch = [
         vmem((width, 3 * inner), BF16),
         vmem((inner, width), BF16),
         vmem((3 * inner, width), BF16),
         vmem((width, inner), BF16),
-        vmem((seq, width), BF16),
+        vmem((2, seq, width), BF16),
         vmem((seq, width), F32),
         vmem((seq, 128), F32),
         vmem((seq, width), BF16),
@@ -618,7 +654,7 @@
         vmem((heads, seq, seq), F32),
         vmem((seq, inner), BF16),
         vmem((seq, width), BF16),
-        vmem((seq, width), BF16),
+        vmem((2, seq, width), BF16),
         vmem((seq, inner), BF16),
         vmem((seq, inner), F32),
         vmem((seq, inner), F32),
@@ -647,16 +683,18 @@
         vmem((side, inner // 2, width // n_dp), BF16),
         vmem((side, inner // 2, width // n_dp), BF16),
         vmem((inner, width // n_dp), BF16),
-        dma((w_blk,)),
-        dma,
+        pltpu.SMEM((1, 8), jnp.int32),
+        dma((6,)),
+        dma((2,)),
+        dma((CHUNKS,)),
         dma((3 + 2 * CHUNKS,)),
         dma((2,)),
         dma((CHUNKS, PIECES)),
         dma((CHUNKS, PIECES)),
         dma((CHUNKS,)),
         dma((CHUNKS,)),
-        dma((6 + CHUNKS, 2, side)),
-        dma((6 + CHUNKS, 2, side)),
+        dma((5 + 2 * CHUNKS, 2, side)),
+        dma((5 + 2 * CHUNKS, 2, side)),
     ]
     shapes = (
         jax.ShapeDtypeStruct((1, seq, width), BF16),
@@ -667,7 +705,7 @@
     results = pl.pallas_call(
         kernel,
         out_shape=shapes,
-        in_specs=[pl.BlockSpec(memory_space=pltpu.SMEM)] + [any_space] * 4,
+        in_specs=[any_space] * 5,
         out_specs=[any_space] * 4,
         scratch_shapes=scratch,
         compiler_params=pltpu.CompilerParams(

time: 152 us -> 142 us (0.934)
  Pallas kernels: 151 us -> 141 us
    pallas_call x1, Pallas kernels: 149 us -> 138 us  [on_device(): pl.pallas_call(kernel, out_shape=shapes, in_specs=[any_space] * 5, out_sp...]
where the time goes in v3:
time: 142 us; the launch traced here: 141 us
  Pallas kernels  141 us (99%)
    pallas_call x1, Pallas kernels, on_device(): pl.pallas_call(kernel, out_shape=shapes, in_specs=[any_space] * 5, out_sp...  138 us

profile of v3, /device:TPU:0, one launch (start us, length us, event | category | flops | bytes accessed | tf_op | source)
XLA Modules:
  0.0 141.4 jit_solution(16748361500674089808)
XLA Ops:
  0.6 138.2 %shard_map.84 = (bf16[1,128,2048]{2,1,0:T(8,128)(2,1)}, bf16[1,128,2048]{2,1,0:T(8,128)(2,1)}, bf16[1,128,3072]{2,1,0:T(8,128)(2,1)}, bf16[1,1024,128]{2,1,0:T(8,128)(2,1)}) custom-call(s32[1,8]{1,0:T(1,128)} %lens_in.1, bf16[128,2048]{1,0:T(8,128)(2,1)} %tok.1, bf16[128,2048]{1,0:T(8,128)(2,1)} %cot.1, bf16[1,2048,3072]{2,1,0:T(8,128)(2,1)} %win.1, ...), custom_call_target="tpu_custom_call" | custom-call | tf_op jit(solution)/shard_map/pallas_call | solution.py:705
  138.8 2.4 %shard_map.85 = (bf16[1,128,2048]{2,1,0:T(8,128)(2,1)}, bf16[1,128,2048]{2,1,0:T(8,128)(2,1)}, bf16[1,128,3072]{2,1,0:T(8,128)(2,1)}, bf16[1,1024,128]{2,1,0:T(8,128)(2,1)}) custom-call(bf16[1,128,2048]{2,1,0:T(8,128)(2,1)} %get-tuple-element.8.refs_0_, bf16[1,128,2048]{2,1,0:T(8,128)(2,1)} %get-tuple-element.9.refs_1_, ...), custom_call_target="tpu_custom_call" | custom-call | tf_op jit(solution)/shard_map/pallas_call | solution.py:715

commit v4 on v3

--- a/solution.py
+++ b/solution.py
@@ -70,22 +70,18 @@
     up4,
     n_x,
     n_z,
-    m_x,
-    m_z,
+    m_f,
     gp_x,
     gp_z,
-    up_x,
-    up_z,
+    up_f,
     p_x,
     p_z,
-    o_x,
-    o_z,
+    o_g,
     r_x,
     r_z,
     s_x,
     s_z,
-    ro_x,
-    ro_z,
+    ro_g,
     go_buf,
     lens,
     win_sem,
@@ -308,6 +304,7 @@
 
     n_kind, m_kind, r_kind, ro_kind, fin_kind, gp_kind = range(6)
     up_kind = gp_kind + CHUNKS
+    late_r_kind = up_kind + CHUNKS
     mine_x, mine_z = aligned(my_x, seq), aligned(my_z, seq)
 
     def dp_copy(src, dst, kind, axis, d):
@@ -326,21 +323,29 @@
             dp_copy(n_t, n_z.at[:, mine_z], n_kind, 1, d),
         )
 
+    odd = lax.rem(sec, 2) == 1
+    my_f = jnp.where(odd, my_z, my_x)
+    my_g = jnp.where(odd, my_x, my_z)
+    mine_f = aligned(my_f, seq)
+
+    def one_copy(src, dst, kind, second, d):
+        return pltpu.make_async_remote_copy(
+            src_ref=src,
+            dst_ref=dst,
+            send_sem=dp_send.at[kind, 0, d],
+            recv_sem=dp_recv.at[kind, 0, d],
+            device_id={"dp": jnp.where(odd != second, at_z(d), at_x(d))},
+            device_id_type=MESH,
+        )
+
     def m_copies(d):
-        return (
-            dp_copy(m_t.at[:half_in], m_x.at[:, mine_x], m_kind, 0, d),
-            dp_copy(m_t.at[half_in:], m_z.at[:, mine_z], m_kind, 1, d),
-        )
+        return (one_copy(m_t, m_f.at[:, mine_f], m_kind, False, d),)
 
     def up_copies(c, d):
-        x, z = lax.rem(my_x + d, side), lax.rem(my_z + d, side)
         rows = pl.ds(c * rows_c, rows_c)
-        to_x = pl.ds(pl.multiple_of(my_x * seq + c * rows_c, rows_c), rows_c)
-        to_z = pl.ds(pl.multiple_of(my_z * seq + c * rows_c, rows_c), rows_c)
-        return (
-            dp_copy(up4.at[:, x, rows], up_x.at[:, to_x], up_kind + c, 0, d),
-            dp_copy(up4.at[z, :, rows], up_z.at[:, to_z], up_kind + c, 1, d),
-        )
+        to = pl.ds(pl.multiple_of(my_f * seq + c * rows_c, rows_c), rows_c)
+        src = up4.at[lax.rem(my_f + d, side), :, rows]
+        return (one_copy(src, up_f.at[:, to], up_kind + c, False, d),)
 
     def gp_copies(c, d):
         x, z = lax.rem(my_x + d, side), lax.rem(my_z + d, side)
@@ -357,28 +362,27 @@
             dp_copy(gp.at[rows, z_cols], gp_z.at[my_z, rows], gp_kind + c, 1, d),
         )
 
-    def r_copies(d):
+    order = (2, 1, 3, 0)
+
+    def r_copies(half, d):
         x, z = lax.rem(my_x + d, side), lax.rem(my_z + d, side)
+        kind = late_r_kind if half else r_kind
+        blocks = pl.ds(2 * half, 2)
         return (
-            dp_copy(p_z.at[x], r_z.at[d], r_kind, 0, d),
-            dp_copy(p_x.at[z], r_x.at[d], r_kind, 1, d),
+            dp_copy(p_z.at[x, blocks], r_z.at[d, blocks], kind, 0, d),
+            dp_copy(p_x.at[z, blocks], r_x.at[d, blocks], kind, 1, d),
         )
 
     def ro_copies(d):
-        x, z = lax.rem(my_x + d, side), lax.rem(my_z + d, side)
-        return (
-            dp_copy(o_z.at[x], ro_z.at[d], ro_kind, 0, d),
-            dp_copy(o_x.at[z], ro_x.at[d], ro_kind, 1, d),
-        )
+        return (one_copy(o_g.at[lax.rem(my_g + d, side)], ro_g.at[d], ro_kind, True, d),)
 
     fin_x = gi.at[0, :, aligned(my_x, gp_cols)]
     fin_z = gi.at[0, :, pl.ds(pl.multiple_of(half_cols + my_z * gp_cols, gp_cols), gp_cols)]
 
     def fin_copies(d):
-        x, z = lax.rem(my_x + d, side), lax.rem(my_z + d, side)
         return (
-            dp_copy(s_x.at[x], fin_x, fin_kind, 0, d),
-            dp_copy(s_z.at[z], fin_z, fin_kind, 1, d),
+            dp_copy(s_x.at[d], fin_x, fin_kind, 0, d),
+            dp_copy(s_z.at[d], fin_z, fin_kind, 1, d),
         )
 
     def start(*pairs):
@@ -400,8 +404,7 @@
             start(n_copies(d), m_copies(d))
         n_x[:, mine_x] = n_t[...]
         n_z[:, mine_z] = n_t[...]
-        m_x[:, mine_x] = m_t[:half_in]
-        m_z[:, mine_z] = m_t[half_in:]
+        m_f[:, mine_f] = m_t[...]
 
     @pl.when(sec < sections - 1)
     def _():
@@ -497,7 +500,9 @@
         bwd_hop(c).start()
         ig_copy(c).start()
         for b in range(n_dp):
-            up4[b // side, b % side, rows] = up[up_slot, rows, b * seq : (b + 1) * seq]
+            f = jnp.where(odd, b // side, b % side)
+            g = jnp.where(odd, b % side, b // side)
+            up4[f, g, rows] = up[up_slot, rows, b * seq : (b + 1) * seq]
         for d in (2, 1, 3):
             start(up_copies(c, d))
 
@@ -508,8 +513,7 @@
     gp_x[my_x] = gp[:, aligned(my_x, gp_cols)]
     gp_z[my_z] = gp[:, pl.ds(pl.multiple_of(half_cols + my_z * gp_cols, gp_cols), gp_cols)]
     for b in range(side):
-        up_x[b, mine_x] = up4[b, my_x]
-        up_z[b, mine_z] = up4[my_z, b]
+        up_f[b, mine_f] = up4[my_f, b]
 
     arrived(n_copies)
     for c in reversed(range(CHUNKS)):
@@ -517,28 +521,28 @@
     group = side * seq
     gx = gp_x[...].reshape(group, gp_cols)
     gz = gp_z[...].reshape(group, gp_cols)
-    for d in (2, 1, 3, 0):
-        x, z = lax.rem(my_x + d, side), lax.rem(my_z + d, side)
-        first = jnp.dot(n_x[aligned(z, quarter), :], gx, preferred_element_type=F32) * grad_scale
-        p_x[z] = first.astype(BF16)
-        if d:
-            r_copies(d)[1].start()
-        for b in range(side):
-            at = pl.ds(pl.multiple_of(b * quarter + x * seq, seq), seq)
-            second = jnp.dot(n_z[at, :], gz, preferred_element_type=F32) * grad_scale
-            p_z[x, b] = second.astype(BF16)
-        if d:
-            r_copies(d)[0].start()
+    for half in (0, 1):
+        for d in order:
+            x, z = lax.rem(my_x + d, side), lax.rem(my_z + d, side)
+            for place in (2 * half, 2 * half + 1):
+                to_x = lax.rem(my_x + order[place], side)
+                to_z = lax.rem(my_z + order[place], side)
+                at_first = pl.ds(pl.multiple_of(z * quarter + to_x * seq, seq), seq)
+                first = jnp.dot(n_x[at_first, :], gx, preferred_element_type=F32)
+                p_x[z, place] = (first * grad_scale).astype(BF16)
+                at_second = pl.ds(pl.multiple_of(to_z * quarter + x * seq, seq), seq)
+                second = jnp.dot(n_z[at_second, :], gz, preferred_element_type=F32)
+                p_z[x, place] = (second * grad_scale).astype(BF16)
+            if d:
+                start(r_copies(half, d))
 
     arrived(m_copies)
     for c in reversed(range(CHUNKS)):
         arrived(lambda d: up_copies(c, d))
     for d in (2, 1, 3, 0):
-        x, z = lax.rem(my_x + d, side), lax.rem(my_z + d, side)
-        first = jnp.dot(m_x[...], up_x[z], preferred_element_type=F32) * grad_scale
-        second = jnp.dot(m_z[...], up_z[x], preferred_element_type=F32) * grad_scale
-        o_x[z] = first.astype(BF16)
-        o_z[x] = second.astype(BF16)
+        g = lax.rem(my_g + d, side)
+        total = jnp.dot(m_f[...], up_f[g], preferred_element_type=F32) * grad_scale
+        o_g[g] = total.astype(BF16)
         if d:
             start(ro_copies(d))
 
@@ -546,41 +550,32 @@
         for d in (1, 3, 2):
             copies(d)[axis].wait_recv()
 
-    landed(r_copies, 1)
-    for b in range(side):
-        at = slice(b * seq, (b + 1) * seq)
-        total = p_x[my_z, at].astype(F32)
-        for d in (1, 2, 3):
-            total = total + r_x[d, at].astype(F32)
-        s_x[b] = total.astype(BF16)
-    for d in (2, 1, 3):
-        fin_copies(d)[0].start()
-    landed(r_copies, 0)
-    for b in range(side):
-        total = p_z[my_x, b].astype(F32)
-        for d in (1, 2, 3):
-            total = total + r_z[d, b].astype(F32)
-        s_z[b] = total.astype(BF16)
-    for d in (2, 1, 3):
-        fin_copies(d)[1].start()
-    own_x = pltpu.make_async_copy(s_x.at[my_x], fin_x, own_sem.at[0])
-    own_z = pltpu.make_async_copy(s_z.at[my_z], fin_z, own_sem.at[1])
+    for half in (0, 1):
+        for axis in (1, 0):
+            landed(lambda d: r_copies(half, d), axis)
+            own, arrivals, sums = (p_x, r_x, s_x) if axis else (p_z, r_z, s_z)
+            for place in (2 * half, 2 * half + 1):
+                total = own[my_z if axis else my_x, place].astype(F32)
+                for d in (1, 2, 3):
+                    total = total + arrivals[d, place].astype(F32)
+                sums[order[place]] = total.astype(BF16)
+                if order[place]:
+                    fin_copies(order[place])[1 - axis].start()
+    own_x = pltpu.make_async_copy(s_x.at[0], fin_x, own_sem.at[0])
+    own_z = pltpu.make_async_copy(s_z.at[0], fin_z, own_sem.at[1])
     own_x.start()
     own_z.start()
 
     arrived(ro_copies)
-    first = o_x[my_z].astype(F32)
-    second = o_z[my_x].astype(F32)
+    total = o_g[my_g].astype(F32)
     for d in (1, 2, 3):
-        first = first + ro_x[d].astype(F32)
-        second = second + ro_z[d].astype(F32)
-    go_buf[:half_in] = first.astype(BF16)
-    go_buf[half_in:] = second.astype(BF16)
+        total = total + ro_g[d].astype(F32)
+    go_buf[...] = total.astype(BF16)
     go_copy = pltpu.make_async_copy(go_buf, go.at[0], local_sem.at[2 + 2 * CHUNKS])
     go_copy.start()
 
     for d in (1, 2, 3):
-        pairs = [n_copies(d), m_copies(d), r_copies(d), ro_copies(d)]
+        pairs = [n_copies(d), m_copies(d), r_copies(0, d), r_copies(1, d), ro_copies(d)]
         pairs += [gp_copies(c, d) for c in range(CHUNKS)]
         pairs += [up_copies(c, d) for c in range(CHUNKS)]
         for pair in pairs:
@@ -666,22 +661,18 @@
         vmem((side, side, seq, width // n_dp), BF16),
         vmem((width, group), BF16),
         vmem((width, group), BF16),
-        vmem((inner // 2, group), BF16),
-        vmem((inner // 2, group), BF16),
+        vmem((inner, group), BF16),
         vmem((side, seq, gp_cols), BF16),
         vmem((side, seq, gp_cols), BF16),
         vmem((side, group, width // n_dp), BF16),
-        vmem((side, group, width // n_dp), BF16),
-        vmem((side, width // side, gp_cols), BF16),
         vmem((side, side, seq, gp_cols), BF16),
-        vmem((side, inner // 2, width // n_dp), BF16),
-        vmem((side, inner // 2, width // n_dp), BF16),
-        vmem((side, width // side, gp_cols), BF16),
+        vmem((side, side, seq, gp_cols), BF16),
+        vmem((side, inner, width // n_dp), BF16),
+        vmem((side, side, seq, gp_cols), BF16),
         vmem((side, side, seq, gp_cols), BF16),
         vmem((side, seq, gp_cols), BF16),
         vmem((side, seq, gp_cols), BF16),
-        vmem((side, inner // 2, width // n_dp), BF16),
-        vmem((side, inner // 2, width // n_dp), BF16),
+        vmem((side, inner, width // n_dp), BF16),
         vmem((inner, width // n_dp), BF16),
         pltpu.SMEM((1, 8), jnp.int32),
         dma((6,)),
@@ -693,8 +684,8 @@
         dma((CHUNKS, PIECES)),
         dma((CHUNKS,)),
         dma((CHUNKS,)),
-        dma((5 + 2 * CHUNKS, 2, side)),
-        dma((5 + 2 * CHUNKS, 2, side)),
+        dma((6 + 2 * CHUNKS, 2, side)),
+        dma((6 + 2 * CHUNKS, 2, side)),
     ]
     shapes = (
         jax.ShapeDtypeStruct((1, seq, width), BF16),

time: 142 us -> 140 us (0.986)
  Pallas kernels: 141 us -> 139 us
    pallas_call x1, Pallas kernels: 138 us -> 136 us  [on_device(): pl.pallas_call(kernel, out_shape=shapes, in_specs=[any_space] * 5, out_sp...]
where the time goes in v4:
time: 140 us; the launch traced here: 139 us
  Pallas kernels  139 us (99%)
    pallas_call x1, Pallas kernels, on_device(): pl.pallas_call(kernel, out_shape=shapes, in_specs=[any_space] * 5, out_sp...  136 us

profile of v4, /device:TPU:0, one launch (start us, length us, event | category | flops | bytes accessed | tf_op | source)
XLA Modules:
  0.0 139.5 jit_solution(17023200053413915951)
XLA Ops:
  0.6 136.2 %shard_map.84 = (bf16[1,128,2048]{2,1,0:T(8,128)(2,1)}, bf16[1,128,2048]{2,1,0:T(8,128)(2,1)}, bf16[1,128,3072]{2,1,0:T(8,128)(2,1)}, bf16[1,1024,128]{2,1,0:T(8,128)(2,1)}) custom-call(s32[1,8]{1,0:T(1,128)} %lens_in.1, bf16[128,2048]{1,0:T(8,128)(2,1)} %tok.1, bf16[128,2048]{1,0:T(8,128)(2,1)} %cot.1, bf16[1,2048,3072]{2,1,0:T(8,128)(2,1)} %win.1, ...), custom_call_target="tpu_custom_call" | custom-call | tf_op jit(solution)/shard_map/pallas_call | solution.py:696
  136.9 2.4 %shard_map.85 = (bf16[1,128,2048]{2,1,0:T(8,128)(2,1)}, bf16[1,128,2048]{2,1,0:T(8,128)(2,1)}, bf16[1,128,3072]{2,1,0:T(8,128)(2,1)}, bf16[1,1024,128]{2,1,0:T(8,128)(2,1)}) custom-call(bf16[1,128,2048]{2,1,0:T(8,128)(2,1)} %get-tuple-element.8.refs_0_, bf16[1,128,2048]{2,1,0:T(8,128)(2,1)} %get-tuple-element.9.refs_1_, ...), custom_call_target="tpu_custom_call" | custom-call | tf_op jit(solution)/shard_map/pallas_call | solution.py:706

commit v5 on v4

--- a/solution.py
+++ b/solution.py
@@ -362,7 +362,7 @@
             dp_copy(gp.at[rows, z_cols], gp_z.at[my_z, rows], gp_kind + c, 1, d),
         )
 
-    order = (2, 1, 3, 0)
+    order = (1, 3, 2, 0)
 
     def r_copies(half, d):
         x, z = lax.rem(my_x + d, side), lax.rem(my_z + d, side)

time: 140 us -> 141 us (level)
    pallas_call x1, Pallas kernels: 136 us -> 138 us  [on_device(): pl.pallas_call(kernel, out_shape=shapes, in_specs=[any_space] * 5, out_sp...]
where the time goes in v5:
time: 141 us
  Pallas kernels  140 us (99%)
    pallas_call x1, Pallas kernels, on_device(): pl.pallas_call(kernel, out_shape=shapes, in_specs=[any_space] * 5, out_sp...  138 us

profile of v5, /device:TPU:0, one launch (start us, length us, event | category | flops | bytes accessed | tf_op | source)
XLA Modules:
  0.0 141.1 jit_solution(12584205940174913265)
XLA Ops:
  0.6 137.9 %shard_map.84 = (bf16[1,128,2048]{2,1,0:T(8,128)(2,1)}, bf16[1,128,2048]{2,1,0:T(8,128)(2,1)}, bf16[1,128,3072]{2,1,0:T(8,128)(2,1)}, bf16[1,1024,128]{2,1,0:T(8,128)(2,1)}) custom-call(s32[1,8]{1,0:T(1,128)} %lens_in.1, bf16[128,2048]{1,0:T(8,128)(2,1)} %tok.1, bf16[128,2048]{1,0:T(8,128)(2,1)} %cot.1, bf16[1,2048,3072]{2,1,0:T(8,128)(2,1)} %win.1, ...), custom_call_target="tpu_custom_call" | custom-call | tf_op jit(solution)/shard_map/pallas_call | solution.py:696
  138.5 2.4 %shard_map.85 = (bf16[1,128,2048]{2,1,0:T(8,128)(2,1)}, bf16[1,128,2048]{2,1,0:T(8,128)(2,1)}, bf16[1,128,3072]{2,1,0:T(8,128)(2,1)}, bf16[1,1024,128]{2,1,0:T(8,128)(2,1)}) custom-call(bf16[1,128,2048]{2,1,0:T(8,128)(2,1)} %get-tuple-element.8.refs_0_, bf16[1,128,2048]{2,1,0:T(8,128)(2,1)} %get-tuple-element.9.refs_1_, ...), custom_call_target="tpu_custom_call" | custom-call | tf_op jit(solution)/shard_map/pallas_call | solution.py:706
